TPU v7x, 512 devices: a whole 4x4x16 slice. The times are simulated.
512 devices in a mesh: gx: 16 (over x, z_lo), gy: 32 (over z_hi, y, core).
Axes of the slice: x: 4, y: 4, z: 16 (z_hi: 4, z_lo: 4; z = z_hi * 4 + z_lo), core: 2. Of those that a mesh axis runs over, the one named last changes fastest.
Arguments:
- snapshot: float32 [512, 512, 384], P('gx', 'gy'), may hold values from -32 to 32
- start_one: float32 [512, 96], replicated, may hold values from -4 to 4
- start_two: float32 [512, 96], replicated, may hold values from -4 to 4
Outputs:
- basis_one: float32 [512, 96], replicated
- basis_two: float32 [512, 96], replicated
- core_tensor: float32 [96, 96, 384], P('gx', 'gy')
All inputs are finite; a program needn't handle non-finite values.
Results may differ from a plain program's by a relative error of at most 0.0003.
Values sent between devices are 32-bit elements; how exact they have to be, the bound alone decides.
A program may use at most 64 MiB of HBM per device.

v0:
```python
import jax
import jax.numpy as jnp
from jax import lax
from jax.sharding import PartitionSpec as P

I2 = 512
CHAN = 12
I3 = 32
RANK = 96
ITERS = 6


precise = lax.Precision.HIGHEST


def normalize(images, cross_gram):
    factor = jnp.linalg.cholesky(cross_gram)
    return lax.linalg.triangular_solve(
        factor, images, left_side=False, lower=True, transpose_a=True
    )


def refine_whole(gram_full, initial):
    vectors = initial
    for sweep_index in range(ITERS):
        images = jnp.dot(gram_full, vectors, precision=precise)
        vectors = normalize(images, jnp.dot(images.T, images, precision=precise))
    return vectors


def body(snapshot, start_one, start_two):
    rows_one = snapshot.shape[0]
    rows_two = snapshot.shape[1]
    scale_one = 1.0 / (I2 * CHAN * I3)
    scale_two = 1.0 / (RANK * CHAN * I3)
    fibers = lax.all_to_all(snapshot, "gx", split_axis=2, concat_axis=0, tiled=True)
    flat_one = fibers.reshape(fibers.shape[0], -1)
    partial_one = jnp.dot(flat_one, flat_one.T, precision=precise)
    gram_one = lax.psum(partial_one, ("gx", "gy")) * scale_one
    basis_one = refine_whole(gram_one, start_one)
    own_basis = lax.dynamic_slice_in_dim(basis_one, lax.axis_index("gx") * rows_one, rows_one, 0)
    picked = own_basis
    owned_part = lax.psum_scatter(
        jnp.einsum("ia,ijr->ajr", picked, snapshot, precision=precise),
        "gx",
        scatter_dimension=0,
        tiled=True,
    )
    fibers_second = lax.all_to_all(owned_part, "gy", split_axis=2, concat_axis=1, tiled=True)
    partial_two = jnp.einsum("ajs,aks->jk", fibers_second, fibers_second, precision=precise)
    gram_two = lax.psum(partial_two, ("gx", "gy")) * scale_two
    basis_two = refine_whole(gram_two, start_two)
    own_second = lax.dynamic_slice_in_dim(basis_two, lax.axis_index("gy") * rows_two, rows_two, 0)
    picked = own_second
    scattered = lax.psum_scatter(
        jnp.einsum("jb,ajr->bar", picked, owned_part, precision=precise),
        "gy",
        scatter_dimension=0,
        tiled=True,
    )
    core_tensor = jnp.transpose(scattered, (1, 0, 2))
    return (basis_one, basis_two, core_tensor)


def solution(mesh):
    in_specs = (P("gx", "gy", None), P(), P())
    out_specs = (P(), P(), P("gx", "gy", None))
    return jax.shard_map(body, mesh=mesh, in_specs=in_specs, out_specs=out_specs, check_vma=False)
```

profile of v0, /device:TPU:1, one launch (start us, length us, event | category | flops | bytes accessed | tf_op | source)
XLA Modules:
  0.0 1474.8 jit_solution(14099317240803533830)
XLA Ops:
  11.8 30.6 %all_to_all.33 = f32[16,1,12288]{2,1,0:T(1,128)S(1)} all-to-all(f32[16,1,12288]{2,1,0:T(1,128)} %reshape.72), channel_id=1, replica_groups=mesh['gx'=16,'gy'=32] {'gx'}, dimensions={0} | all-to-all | bytes 1572864 | tf_op jit(solution)/shard_map/all_to_all | solution.py:36
  57.9 467.4 %all-reduce.4.cloned.1.call-done = f32[512,512]{1,0:T(8,128)} async-done(((f32[512,512]{1,0:T(8,128)}), f32[512,512]{1,0:T(8,128)}) %all-reduce.4.cloned.1.call-update) | async-done | bytes 1048592 | tf_op jit(solution)/shard_map/psum | solution.py:39
  528.3 8.8 cholesky.194
  538.4 7.4 custom-call.16
  547.7 8.8 cholesky.205
  557.9 7.4 custom-call.17
  567.2 9.2 cholesky.216
  577.7 7.4 custom-call.18
  587.1 8.8 cholesky.227
  597.2 7.4 custom-call.19
  606.5 8.8 cholesky.238
  616.7 7.5 custom-call.20
  626.2 8.8 cholesky.249
  649.0 84.5 %reduce-scatter.5.cloned.1.call-done = f32[6,16,384]{2,1,0:T(8,128)} async-done(((f32[96,16,384]{2,1,0:T(8,128)}), f32[6,16,384]{2,1,0:T(8,128)}) %reduce-scatter.5.cloned.1.call-update) | async-done | bytes 147472 | tf_op jit(solution)/shard_map/reduce_scatter | solution.py:43
  735.6 39.5 %all_to_all.34 = f32[32,1,1152]{2,1,0:T(1,128)S(1)} all-to-all(f32[32,1,1152]{2,1,0:T(1,128)S(1)} %reshape.74), channel_id=1, replica_groups=mesh['gx'=16,'gy'=32] {'gy'}, dimensions={0} | all-to-all | bytes 294912 | tf_op jit(solution)/shard_map/all_to_all | solution.py:49
  780.8 456.4 %all-reduce.6.cloned.1.call-done = f32[512,512]{1,0:T(8,128)} async-done(((f32[512,512]{1,0:T(8,128)}), f32[512,512]{1,0:T(8,128)}) %all-reduce.6.cloned.1.call-update) | async-done | bytes 1048592 | tf_op jit(solution)/shard_map/psum | solution.py:51
  1240.1 8.8 cholesky.260
  1259.6 8.8 cholesky.271
  1279.1 8.9 cholesky.282
  1298.7 8.8 cholesky.293
  1318.2 8.8 cholesky.304
  1328.3 7.5 custom-call.26
  1337.8 8.8 cholesky.315
  1358.2 108.5 %reduce-scatter.7.cloned.1.call-done = f32[3,6,384]{2,1,0:T(8,128)} async-done(((f32[96,6,384]{2,1,0:T(8,128)}), f32[3,6,384]{2,1,0:T(8,128)}) %reduce-scatter.7.cloned.1.call-update) | async-done | bytes 27664
  (146 shorter events, 122.7 us)
Async XLA Ops:
  7.2 518.2 %copy-start = (f32[512,96]{0,1:T(8,128)S(1)}, f32[512,96]{0,1:T(8,128)}, u32[]{:S(2)}) copy-start(f32[512,96]{0,1:T(8,128)} %param.7) | copy-start | bytes 589828
  7.2 518.1 %all-reduce.4.cloned.1.call-start = ((), (), s32[]{:S(2)}) async-start(), calls=%async_computation.4 | async-start | bytes 2097152 | tf_op jit(solution)/shard_map/psum | solution.py:39
  57.7 675.8 %reduce-scatter.5.cloned.1.call-start = ((), (), s32[]{:S(2)}) async-start(), calls=%async_computation.5 | async-start | bytes 2506752 | tf_op jit(solution)/shard_map/reduce_scatter | solution.py:43
  525.3 20.8 %copy-start.1 = (f32[512,512]{1,0:T(8,128)S(1)}, f32[512,512]{1,0:T(8,128)}, u32[]{:S(2)}) copy-start(f32[512,512]{1,0:T(8,128)} %all-reduce.4.cloned.1.call-done) | copy-start | bytes 3145732
  606.1 37.9 %copy-start.3 = (f32[32,16,384]{2,1,0:T(8,128)S(1)}, f32[32,16,384]{2,1,0:T(8,128)}, u32[]{:S(2)}) copy-start(f32[32,16,384]{2,1,0:T(8,128)} %param.6) | copy-start | bytes 2359300
  644.0 4.9 copy-start.5
  648.9 588.3 %all-reduce.6.cloned.1.call-start = ((), (), s32[]{:S(2)}) async-start(), calls=%async_computation.6 | async-start | bytes 2097152 | tf_op jit(solution)/shard_map/psum | solution.py:51
  777.5 459.7 %copy-start.7 = (f32[512,96]{0,1:T(8,128)S(1)}, f32[512,96]{0,1:T(8,128)}, u32[]{:S(2)}) copy-start(f32[512,96]{0,1:T(8,128)} %param.8) | copy-start | bytes 589828
  780.3 686.3 %reduce-scatter.7.cloned.1.call-start = ((), (), s32[]{:S(2)}) async-start(), calls=%async_computation.7 | async-start | bytes 1216512
  1237.2 20.8 %copy-start.2 = (f32[512,512]{1,0:T(8,128)S(1)}, f32[512,512]{1,0:T(8,128)}, u32[]{:S(2)}) copy-start(f32[512,512]{1,0:T(8,128)} %all-reduce.6.cloned.1.call-done) | copy-start | bytes 3145732
  1317.7 37.9 %copy-start.4 = (f32[6,16,384]{2,1,0:T(8,128)S(1)}, f32[6,16,384]{2,1,0:T(8,128)}, u32[]{:S(2)}) copy-start(f32[6,16,384]{2,1,0:T(8,128)} %reduce-scatter.5.cloned.1.call-done) | copy-start | bytes 442372
  1355.7 112.4 %copy-start.6 = (f32[512,96]{0,1:T(8,128)}, f32[512,96]{0,1:T(8,128)S(1)}, u32[]{:S(2)}) copy-start(f32[512,96]{0,1:T(8,128)S(1)} %convolution_bitcast_fusion.1) | copy-start | bytes 589828
Sparse Core Ops, SparseCore 0:
  57.8 467.4 all-reduce.3
  649.0 84.4 reduce-scatter.4
  780.5 456.6 all-reduce.5
  1358.3 108.3 reduce-scatter.6
where the time goes:
time: 1480 us; the launch traced here: 1470 us
  waiting for transfers between devices  1120 us (76%)
  other arithmetic  215 us (15%)
  blocking collectives  70.1 us (5%)
  matrix products  32.9 us (2%)
  local copies, waits for them, and re-layouts  24.2 us (2%)
  between operations  14.8 us (1%)
    psum x1, waiting for transfers between devices, body(): gram_one = lax.psum(partial_one, ('gx', 'gy')) * scale_one  467 us
    psum x1, waiting for transfers between devices, body(): gram_two = lax.psum(partial_two, ('gx', 'gy')) * scale_two  456 us
    another operation x36, other arithmetic, normalize(): factor = jnp.linalg.cholesky(cross_gram)  114 us
    unnamed x5, waiting for transfers between devices  109 us
    another operation x24, other arithmetic, normalize(): lax.linalg.triangular_solve(factor, images, left_side=False, lower=True,...  96.4 us
    reduce_scatter x1, waiting for transfers between devices, body(): lax.psum_scatter(jnp.einsum('ia,ijr->ajr', picked, snapshot, precision=pr...  84.5 us
    all_to_all x1, blocking collectives, body(): lax.all_to_all(owned_part, 'gy', split_axis=2, concat_axis=1, tiled=True)  39.5 us
    all_to_all x1, blocking collectives, body(): lax.all_to_all(snapshot, 'gx', split_axis=2, concat_axis=0, tiled=True)  30.6 us
  transfers between devices with their start and end apart: 4, of which 4 were waited for; matrix products, arithmetic and copies ran while one was open for 0% of the time, Pallas kernels for 0%

commit v1 on v0

v1 whole, which is shorter than its diff:
```python
import functools

import jax
import jax.numpy as jnp
from jax import lax
from jax.experimental import pallas as pl
from jax.experimental.pallas import tpu as pltpu
from jax.sharding import PartitionSpec as P

I1 = 512
I2 = 512
COLS = 384
RANK = 96
ITERS = 6
GX = 16
GY = 32
NX = 4
NY = 4
NZ = 16
BLOCKS = [(p, q) for p in range(4) for q in range(p, 4)]
GROWS = 128 * len(BLOCKS)
HALF = GROWS // 2
PIECE = HALF // 16
OWNERS = (0, 3, 6, 9, 12)
COLS_TWO = 6 * COLS // GY

MESH = pl.DeviceIdType.MESH
precise = lax.Precision.HIGHEST


def place():
    gx = lax.axis_index("gx")
    gy = lax.axis_index("gy")
    x, z_lo = lax.div(gx, 4), lax.rem(gx, 4)
    z_hi = lax.div(gy, 8)
    y = lax.rem(lax.div(gy, 2), 4)
    core = lax.rem(gy, 2)
    return gx, gy, x, y, z_hi, z_lo, core


def remote(src, dst, send, recv, target):
    return pltpu.make_async_remote_copy(
        src_ref=src, dst_ref=dst, send_sem=send, recv_sem=recv, device_id=target, device_id_type=MESH
    )


def gx_peer(d):
    gx, gy = place()[:2]
    return (lax.rem(gx + d, GX), gy)


def gy_peer(d):
    gx, gy = place()[:2]
    return (gx, lax.rem(gy + d, GY))


def sibling():
    gx, gy, *_, core = place()
    return (gx, gy + 1 - 2 * core)


def xy_peer(dx, dy):
    gx, gy, x, y, z_hi, z_lo, core = place()
    px, py = lax.rem(x + dx, NX), lax.rem(y + dy, NY)
    return (px * 4 + z_lo, z_hi * 8 + py * 2 + core), px * 4 + py


def z_peer(z):
    gx, gy, x, y, z_hi, z_lo, core = place()
    return (x * 4 + z % 4, (z // 4) * 8 + y * 2 + core)


def zz_peer(dh, dl):
    gx, gy, x, y, z_hi, z_lo, core = place()
    return (x * 4 + lax.rem(z_lo + dl, 4), lax.rem(z_hi + dh, 4) * 8 + y * 2 + core)


def meet(peers):
    barrier = pltpu.get_barrier_semaphore()
    for peer in peers:
        pl.semaphore_signal(barrier, inc=1, device_id=peer, device_id_type=MESH)
    pl.semaphore_wait(barrier, len(peers))


XY = [(dx, dy) for dx in range(NX) for dy in range(NY) if (dx, dy) != (0, 0)]


def all_reduce(gp, total, s):
    gx, gy, x, y, z_hi, z_lo, core = place()
    z = z_hi * 4 + z_lo
    mine = pl.multiple_of(core * HALF, 8)
    other = pl.multiple_of((1 - core) * HALF, 8)
    done = []
    copy = remote(gp.at[pl.ds(other, HALF)], s["rc"], s["c1s"], s["c1r"], sibling())
    copy.start()
    copy.wait_recv()
    done.append(copy)
    s["h"][...] = gp[pl.ds(mine, HALF)] + s["rc"][...]
    copies = []
    for o, (dx, dy) in enumerate(XY):
        peer, q = xy_peer(dx, dy)
        copy = remote(
            s["h"].at[pl.ds(pl.multiple_of(q * PIECE, 8), PIECE)],
            s["rxy"].at[o], s["x1s"].at[o], s["x1r"].at[o], peer,
        )
        copy.start()
        copies.append(copy)
    me = x * 4 + y
    acc = s["h"][pl.ds(pl.multiple_of(me * PIECE, 8), PIECE)]
    for o, copy in enumerate(copies):
        copy.wait_recv()
        acc = acc + s["rxy"][o]
    s["acc"][...] = acc
    done += copies
    def rows(w):
        return pl.ds(8 * w, 8)

    def to_owner(w):
        zw = OWNERS[w]
        return remote(s["acc"].at[rows(w)], s["rz"].at[z], s["z1s"].at[w], s["z1r"].at[z], z_peer(zw))

    def from_owner(w, target):
        return remote(s["agz"].at[rows(w)], s["agz"].at[rows(w)], s["z2s"].at[target], s["z2r"].at[w], z_peer(target))

    for w, zw in enumerate(OWNERS):
        @pl.when(z != zw)
        def _(w=w):
            to_owner(w).start()
    for w, zw in enumerate(OWNERS):
        @pl.when(z == zw)
        def _(w=w, zw=zw):
            part = s["acc"][rows(w)]
            others = [i for i in range(NZ) if i != zw]
            for i in others:
                remote(s["acc"].at[rows(w)], s["rz"].at[i], s["z1s"].at[w], s["z1r"].at[i], z_peer(i)).wait_recv()
                part = part + s["rz"][i]
            s["agz"][rows(w)] = part
            for i in others:
                from_owner(w, i).start()
    for w, zw in enumerate(OWNERS):
        @pl.when(z != zw)
        def _(w=w, zw=zw):
            from_owner(w, zw).wait_recv()
    own = pl.ds(pl.multiple_of(mine + me * PIECE, 8), PIECE)
    copies = []
    for o, (dx, dy) in enumerate(XY):
        peer, q = xy_peer(dx, dy)
        copy = remote(s["agz"], total.at[own], s["x2s"].at[o], s["x2r"].at[o], peer)
        copy.start()
        copies.append(copy)
    total[own] = s["agz"][...]
    for copy in copies:
        copy.wait_recv()
    done += copies
    copy = remote(total.at[pl.ds(mine, HALF)], total.at[pl.ds(mine, HALF)], s["c2s"], s["c2r"], sibling())
    copy.start()
    copy.wait_recv()
    done.append(copy)
    for copy in done:
        copy.wait_send()
    for w, zw in enumerate(OWNERS):
        @pl.when(z != zw)
        def _(w=w):
            to_owner(w).wait_send()

        @pl.when(z == zw)
        def _(w=w, zw=zw):
            for i in range(NZ):
                if i != zw:
                    from_owner(w, i).wait_send()


DMA = pltpu.SemaphoreType.DMA
REDUCE = dict(
    gp=pltpu.VMEM((GROWS, 128), jnp.float32),
    total=pltpu.VMEM((GROWS, 128), jnp.float32),
    rc=pltpu.VMEM((HALF, 128), jnp.float32),
    h=pltpu.VMEM((HALF, 128), jnp.float32),
    rxy=pltpu.VMEM((15, PIECE, 128), jnp.float32),
    acc=pltpu.VMEM((PIECE, 128), jnp.float32),
    rz=pltpu.VMEM((NZ, 8, 128), jnp.float32),
    agz=pltpu.VMEM((PIECE, 128), jnp.float32),
    c1s=DMA, c1r=DMA, c2s=DMA, c2r=DMA,
    x1s=DMA((15,)), x1r=DMA((15,)), x2s=DMA((15,)), x2r=DMA((15,)),
    z1s=DMA((5,)), z1r=DMA((NZ,)), z2s=DMA((NZ,)), z2r=DMA((5,)),
)


def gram_blocks(flat, gp):
    n = 0
    for p in range(4):
        strip = lax.dot_general(
            flat[128 * p : 128 * (p + 1)], flat[128 * p :], (((1,), (1,)), ((), ())),
            precision=precise, preferred_element_type=jnp.float32,
        )
        for q in range(4 - p):
            gp[128 * n : 128 * (n + 1)] = strip[:, 128 * q : 128 * (q + 1)]
            n += 1


def reduce_peers():
    peers = [xy_peer(dx, dy)[0] for dx in range(1, NX) for dy in range(1, NY)]
    return peers + [zz_peer(a, b) for a in range(1, 4) for b in range(1, 4)]


def first_kernel(x_ref, fib_ref, g_ref, scratch):
    s = scratch
    gx, gy, *_ = place()
    meet([gx_peer(d) for d in range(1, GX)] + [gy_peer(d) for d in range(1, GY)] + reduce_peers())
    for j in range(GX):
        s["xs"][j] = x_ref[:, j, :]
    copies = []
    for d in range(1, GX):
        peer = gx_peer(d)
        copy = remote(s["xs"].at[peer[0]], s["fib"].at[gx], s["as"].at[d - 1], s["ar"].at[d - 1], peer)
        copy.start()
        copies.append(copy)
    s["fib"][gx] = s["xs"][gx]
    for copy in copies:
        copy.wait_recv()
    flat = s["fib"][...].reshape(I1, COLS)
    fib_ref[...] = flat
    gram_blocks(flat, s["gp"])
    all_reduce(s["gp"], s["total"], s)
    g_ref[...] = s["total"][...]
    for copy in copies:
        copy.wait_send()


def second_kernel(bt_ref, fib_ref, f2_ref, g_ref, scratch):
    s = scratch
    gx, gy, *_ = place()
    meet([gx_peer(d) for d in range(1, GX)] + [gy_peer(d) for d in range(1, GY)] + reduce_peers())
    shrunk = lax.dot_general(
        bt_ref[...], fib_ref[...], (((1,), (0,)), ((), ())), precision=precise, preferred_element_type=jnp.float32
    )
    for g in range(GX):
        s["ss"][g, 0:6] = shrunk[6 * g : 6 * (g + 1)]
        s["ss"][g, 6:8] = jnp.zeros((2, COLS), jnp.float32)
    copies = []
    for d in range(1, GX):
        peer = gx_peer(d)
        copy = remote(s["ss"].at[peer[0]], s["rs"].at[gx], s["as"].at[d - 1], s["ar"].at[d - 1], peer)
        copy.start()
        copies.append(copy)
    s["rs"][gx] = s["ss"][gx]
    for copy in copies:
        copy.wait_recv()
    wide = jnp.concatenate([s["rs"][:, a, :] for a in range(6)], axis=1)
    pad = jnp.zeros((GX, 128 - COLS_TWO), jnp.float32)
    for u in range(GY):
        s["st"][u] = jnp.concatenate([wide[:, COLS_TWO * u : COLS_TWO * (u + 1)], pad], axis=1)
    seconds = []
    for d in range(1, GY):
        peer = gy_peer(d)
        copy = remote(s["st"].at[peer[1]], s["f2"].at[gy], s["bs"].at[d - 1], s["br"].at[d - 1], peer)
        copy.start()
        seconds.append(copy)
    s["f2"][gy] = s["st"][gy]
    for copy in seconds:
        copy.wait_recv()
    flat = s["f2"][...].reshape(I2, 128)
    f2_ref[...] = flat
    gram_blocks(flat, s["gp"])
    all_reduce(s["gp"], s["total"], s)
    g_ref[...] = s["total"][...]
    for copy in copies + seconds:
        copy.wait_send()


def third_kernel(bt_ref, f2_ref, out_ref, scratch):
    s = scratch
    gx, gy, *_ = place()
    meet([gy_peer(d) for d in range(1, GY)])
    core = lax.dot_general(
        bt_ref[...], f2_ref[...], (((1,), (0,)), ((), ())), precision=precise, preferred_element_type=jnp.float32
    )
    for u in range(GY):
        s["cs"][u, 0:3] = core[3 * u : 3 * (u + 1)]
        s["cs"][u, 3:8] = jnp.zeros((5, 128), jnp.float32)
    copies = []
    for d in range(1, GY):
        peer = gy_peer(d)
        copy = remote(s["cs"].at[peer[1]], s["rc"].at[gy], s["bs"].at[d - 1], s["br"].at[d - 1], peer)
        copy.start()
        copies.append(copy)
    s["rc"][gy] = s["cs"][gy]
    for copy in copies:
        copy.wait_recv()
    wide = jnp.concatenate([s["rc"][u][:, :COLS_TWO] for u in range(GY)], axis=1)
    for a in range(6):
        out_ref[a] = wide[0:3, COLS * a : COLS * (a + 1)]
    for copy in copies:
        copy.wait_send()


FIRST = REDUCE | dict(
    xs=pltpu.VMEM((GX, 32, COLS), jnp.float32), fib=pltpu.VMEM((GX, 32, COLS), jnp.float32),
    **{"as": DMA((15,)), "ar": DMA((15,))},
)
SECOND = REDUCE | dict(
    ss=pltpu.VMEM((GX, 8, COLS), jnp.float32), rs=pltpu.VMEM((GX, 8, COLS), jnp.float32),
    st=pltpu.VMEM((GY, GX, 128), jnp.float32), f2=pltpu.VMEM((GY, GX, 128), jnp.float32),
    bs=DMA((31,)), br=DMA((31,)), **{"as": DMA((15,)), "ar": DMA((15,))},
)
THIRD = dict(
    cs=pltpu.VMEM((GY, 8, 128), jnp.float32), rc=pltpu.VMEM((GY, 8, 128), jnp.float32),
    bs=DMA((31,)), br=DMA((31,)),
)

VMEM = pl.BlockSpec(memory_space=pltpu.VMEM)


def exchange(kernel, name, ident, outs, scratch):
    def body(*refs):
        count = len(refs) - 1
        kernel(*refs[:count], refs[count])

    def call(*args):
        single = len(outs) == 1
        shapes = [jax.ShapeDtypeStruct(o, jnp.float32) for o in outs]
        return pl.pallas_call(
            body,
            out_shape=shapes[0] if single else shapes,
            in_specs=[VMEM] * len(args),
            out_specs=VMEM if single else [VMEM] * len(outs),
            scratch_shapes=[scratch],
            compiler_params=pltpu.CompilerParams(
                collective_id=ident, has_side_effects=True, vmem_limit_bytes=32 * 1024 * 1024
            ),
            name=name,
        )(*args)

    return call


def normalize(images, cross_gram):
    factor = jnp.linalg.cholesky(cross_gram)
    return lax.linalg.triangular_solve(
        factor, images, left_side=False, lower=True, transpose_a=True
    )


def refine_whole(gram_full, initial):
    vectors = initial
    for sweep_index in range(ITERS):
        images = jnp.dot(gram_full, vectors, precision=precise)
        vectors = normalize(images, jnp.dot(images.T, images, precision=precise))
    return vectors


def whole(blocks, scale):
    b = {}
    for n, (p, q) in enumerate(BLOCKS):
        block = blocks[128 * n : 128 * (n + 1)] * scale
        b[p, q] = block
        if p != q:
            b[q, p] = block.T
    return jnp.concatenate([jnp.concatenate([b[p, q] for q in range(4)], axis=1) for p in range(4)], axis=0)


def body(snapshot, start_one, start_two):
    fibers, blocks = exchange(first_kernel, "first", 0, [(I1, COLS), (GROWS, 128)], FIRST)(snapshot)
    basis_one = refine_whole(whole(blocks, 1.0 / (I2 * COLS)), start_one)
    fibers_two, blocks = exchange(second_kernel, "second", 1, [(I2, 128), (GROWS, 128)], SECOND)(basis_one.T, fibers)
    basis_two = refine_whole(whole(blocks, 1.0 / (RANK * COLS)), start_two)
    core_tensor = exchange(third_kernel, "third", 2, [(6, 3, COLS)], THIRD)(basis_two.T, fibers_two)
    return (basis_one, basis_two, core_tensor)


def solution(mesh):
    in_specs = (P("gx", "gy", None), P(), P())
    out_specs = (P(), P(), P("gx", "gy", None))
    return jax.shard_map(body, mesh=mesh, in_specs=in_specs, out_specs=out_specs, check_vma=False)
```

time: 1480 us -> 401 us (0.27)
  waiting for transfers between devices: 1120 us -> 0 us
  Pallas kernels: 0 us -> 157 us
  blocking collectives: 70.1 us -> 0 us
  local copies, waits for them, and re-layouts: 24.2 us -> 4.87 us
    psum x2 -> x0, waiting for transfers between devices: 924 us -> none  [the longest x1 467 us: body(): gram_one = lax.psum(partial_one, ('gx', 'gy')) * scale_one]
    pallas_call x0 -> x3, Pallas kernels: none -> 157 us  [call(): pl.pallas_call(body, out_shape=shapes[0] if single else shapes, in_specs=...]
    unnamed x5 -> x0, waiting for transfers between devices: 109 us -> none
    reduce_scatter x1 -> x0, waiting for transfers between devices: 84.5 us -> none  [body(): lax.psum_scatter(jnp.einsum('ia,ijr->ajr', picked, snapshot, precision=pr...]
    all_to_all x2 -> x0, blocking collectives: 70.1 us -> none  [the longest x1 39.5 us: body(): lax.all_to_all(owned_part, 'gy', split_axis=2, concat_axis=1, tiled=True)]
  transfers between devices with their start and end apart: 4 -> 0, of which waited for: 4 -> 0; matrix products, arithmetic and copies ran while one was open for 0% -> 0% of each run, Pallas kernels for 0% -> 0%
where the time goes in v1:
time: 401 us; the launch traced here: 397 us
  other arithmetic  211 us (53%)
  Pallas kernels  157 us (39%)
  matrix products  22.5 us (6%)
  local copies, waits for them, and re-layouts  4.87 us (1%)
    pallas_call x3, Pallas kernels, call(): pl.pallas_call(body, out_shape=shapes[0] if single else shapes, in_specs=...  157 us
    another operation x36, other arithmetic, normalize(): factor = jnp.linalg.cholesky(cross_gram)  114 us
    another operation x24, other arithmetic, normalize(): lax.linalg.triangular_solve(factor, images, left_side=False, lower=True,...  96.3 us
    dot_general x12, matrix products, refine_whole(): images = jnp.dot(gram_full, vectors, precision=precise)  13.8 us

profile of v1, /device:TPU:1, one launch (start us, length us, event | category | flops | bytes accessed | tf_op | source)
XLA Modules:
  0.0 397.3 jit_solution(2392454947799908150)
XLA Ops:
  1.8 71.7 %first.1 = (f32[512,384]{1,0:T(8,128)S(1)}, f32[1280,128]{1,0:T(8,128)S(1)}) custom-call(f32[32,16,384]{2,1,0:T(8,128)S(1)} %copy-done.1), custom_call_target="tpu_custom_call" | custom-call | tf_op jit(solution)/shard_map/first/pallas_call | solution.py:322
  76.0 8.8 %cholesky.194 = f32[96,96]{1,0:T(8,128)S(1)} custom-call(f32[96,96]{1,0:T(8,128)S(1)} %fusion.37), custom_call_target="Cholesky" | custom-call | tf_op jit(solution)/shard_map/jit(cholesky)/cholesky | solution.py:338
  86.1 7.4 %custom-call.16 = f32[1,96,96]{1,2,0:T(8,128)S(1)} custom-call(f32[1,96,96]{2,1,0:T(8,128)S(1)} %fusion), custom_call_target="InvertDiagBlocksLowerTriangular" | custom-call | tf_op jit(solution)/shard_map/triangular_solve/custom-call.0 | solution.py:339
  95.5 8.8 %cholesky.205 = f32[96,96]{1,0:T(8,128)S(1)} custom-call(f32[96,96]{1,0:T(8,128)S(1)} %fusion.35), custom_call_target="Cholesky" | custom-call | tf_op jit(solution)/shard_map/jit(cholesky)/cholesky | solution.py:338
  105.6 7.4 %custom-call.17 = f32[1,96,96]{1,2,0:T(8,128)S(1)} custom-call(f32[1,96,96]{2,1,0:T(8,128)S(1)} %fusion.1), custom_call_target="InvertDiagBlocksLowerTriangular" | custom-call | tf_op jit(solution)/shard_map/triangular_solve/custom-call.0 | solution.py:339
  114.9 9.3 %cholesky.216 = f32[96,96]{1,0:T(8,128)S(1)} custom-call(f32[96,96]{1,0:T(8,128)S(1)} %fusion.33), custom_call_target="Cholesky" | custom-call | tf_op jit(solution)/shard_map/jit(cholesky)/cholesky | solution.py:338
  125.5 7.4 %custom-call.18 = f32[1,96,96]{1,2,0:T(8,128)S(1)} custom-call(f32[1,96,96]{2,1,0:T(8,128)S(1)} %fusion.2), custom_call_target="InvertDiagBlocksLowerTriangular" | custom-call | tf_op jit(solution)/shard_map/triangular_solve/custom-call.0 | solution.py:339
  134.9 8.8 %cholesky.227 = f32[96,96]{1,0:T(8,128)S(1)} custom-call(f32[96,96]{1,0:T(8,128)S(1)} %fusion.31), custom_call_target="Cholesky" | custom-call | tf_op jit(solution)/shard_map/jit(cholesky)/cholesky | solution.py:338
  145.0 7.4 %custom-call.19 = f32[1,96,96]{1,2,0:T(8,128)S(1)} custom-call(f32[1,96,96]{2,1,0:T(8,128)S(1)} %fusion.3), custom_call_target="InvertDiagBlocksLowerTriangular" | custom-call | tf_op jit(solution)/shard_map/triangular_solve/custom-call.0 | solution.py:339
  154.3 8.8 %cholesky.238 = f32[96,96]{1,0:T(8,128)S(1)} custom-call(f32[96,96]{1,0:T(8,128)S(1)} %fusion.29), custom_call_target="Cholesky" | custom-call | tf_op jit(solution)/shard_map/jit(cholesky)/cholesky | solution.py:338
  164.4 7.5 %custom-call.20 = f32[1,96,96]{1,2,0:T(8,128)S(1)} custom-call(f32[1,96,96]{2,1,0:T(8,128)S(1)} %fusion.4), custom_call_target="InvertDiagBlocksLowerTriangular" | custom-call | tf_op jit(solution)/shard_map/triangular_solve/custom-call.0 | solution.py:339
  173.9 8.8 %cholesky.249 = f32[96,96]{1,0:T(8,128)S(1)} custom-call(f32[96,96]{1,0:T(8,128)S(1)} %fusion.27), custom_call_target="Cholesky" | custom-call | tf_op jit(solution)/shard_map/jit(cholesky)/cholesky | solution.py:338
  184.0 7.4 %custom-call.21 = f32[1,96,96]{1,2,0:T(8,128)S(1)} custom-call(f32[1,96,96]{2,1,0:T(8,128)S(1)} %fusion.5), custom_call_target="InvertDiagBlocksLowerTriangular" | custom-call | tf_op jit(solution)/shard_map/triangular_solve/custom-call.0 | solution.py:339
  191.8 65.8 %second.1 = (f32[512,128]{1,0:T(8,128)S(1)}, f32[1280,128]{1,0:T(8,128)S(1)}) custom-call(f32[96,512]{1,0:T(8,128)S(1)} %fusion.25.refs_0_, f32[512,384]{1,0:T(8,128)S(1)} %get-tuple-element.10.refs_1_), custom_call_target="tpu_custom_call" | custom-call | tf_op jit(solution)/shard_map/second/pallas_call | solution.py:322
  261.0 8.8 %cholesky.260 = f32[96,96]{1,0:T(8,128)S(1)} custom-call(f32[96,96]{1,0:T(8,128)S(1)} %fusion.24), custom_call_target="Cholesky" | custom-call | tf_op jit(solution)/shard_map/jit(cholesky)/cholesky | solution.py:338
  271.1 7.4 %custom-call.22 = f32[1,96,96]{1,2,0:T(8,128)S(1)} custom-call(f32[1,96,96]{2,1,0:T(8,128)S(1)} %fusion.6), custom_call_target="InvertDiagBlocksLowerTriangular" | custom-call | tf_op jit(solution)/shard_map/triangular_solve/custom-call.0 | solution.py:339
  280.4 8.8 %cholesky.271 = f32[96,96]{1,0:T(8,128)S(1)} custom-call(f32[96,96]{1,0:T(8,128)S(1)} %fusion.22), custom_call_target="Cholesky" | custom-call | tf_op jit(solution)/shard_map/jit(cholesky)/cholesky | solution.py:338
  290.5 7.4 %custom-call.23 = f32[1,96,96]{1,2,0:T(8,128)S(1)} custom-call(f32[1,96,96]{2,1,0:T(8,128)S(1)} %fusion.7), custom_call_target="InvertDiagBlocksLowerTriangular" | custom-call | tf_op jit(solution)/shard_map/triangular_solve/custom-call.0 | solution.py:339
  300.3 8.8 %cholesky.282 = f32[96,96]{1,0:T(8,128)S(1)} custom-call(f32[96,96]{1,0:T(8,128)S(1)} %fusion.20), custom_call_target="Cholesky" | custom-call | tf_op jit(solution)/shard_map/jit(cholesky)/cholesky | solution.py:338
  310.4 7.4 %custom-call.24 = f32[1,96,96]{1,2,0:T(8,128)S(1)} custom-call(f32[1,96,96]{2,1,0:T(8,128)S(1)} %fusion.8), custom_call_target="InvertDiagBlocksLowerTriangular" | custom-call | tf_op jit(solution)/shard_map/triangular_solve/custom-call.0 | solution.py:339
  319.7 8.8 %cholesky.293 = f32[96,96]{1,0:T(8,128)S(1)} custom-call(f32[96,96]{1,0:T(8,128)S(1)} %fusion.18), custom_call_target="Cholesky" | custom-call | tf_op jit(solution)/shard_map/jit(cholesky)/cholesky | solution.py:338
  339.2 8.9 %cholesky.304 = f32[96,96]{1,0:T(8,128)S(1)} custom-call(f32[96,96]{1,0:T(8,128)S(1)} %fusion.16), custom_call_target="Cholesky" | custom-call | tf_op jit(solution)/shard_map/jit(cholesky)/cholesky | solution.py:338
  358.8 8.8 %cholesky.315 = f32[96,96]{1,0:T(8,128)S(1)} custom-call(f32[96,96]{1,0:T(8,128)S(1)} %fusion.14), custom_call_target="Cholesky" | custom-call | tf_op jit(solution)/shard_map/jit(cholesky)/cholesky | solution.py:338
  376.7 19.8 %third.1 = f32[6,3,384]{2,1,0:T(4,128)S(1)} custom-call(f32[96,512]{1,0:T(8,128)S(1)} %fusion.12.refs_0_, f32[512,128]{1,0:T(8,128)S(1)} %get-tuple-element.12.refs_1_), custom_call_target="tpu_custom_call" | custom-call | tf_op jit(solution)/shard_map/third/pallas_call | solution.py:322
  (128 shorter events, 65.9 us)
Async XLA Ops:
  0.6 73.8 %copy-start = (f32[512,96]{0,1:T(8,128)S(1)}, f32[512,96]{0,1:T(8,128)}, u32[]{:S(2)}) copy-start(f32[512,96]{0,1:T(8,128)} %param.7) | copy-start | bytes 589828
  0.6 1.2 copy-start.1
  191.8 65.9 %copy-start.3 = (f32[96,512]{1,0:T(8,128)}, f32[96,512]{1,0:T(8,128)S(1)}, u32[]{:S(2)}) copy-start(f32[96,512]{1,0:T(8,128)S(1)} %fusion.25.refs_0_) | copy-start | bytes 589828
  258.4 0.9 copy-start.4
  376.7 19.8 %copy-start.2 = (f32[96,512]{1,0:T(8,128)}, f32[96,512]{1,0:T(8,128)S(1)}, u32[]{:S(2)}) copy-start(f32[96,512]{1,0:T(8,128)S(1)} %fusion.12.refs_0_) | copy-start | bytes 589828

commit v2 on v1

--- a/solution.py
+++ b/solution.py
@@ -334,38 +334,98 @@
     return call
 
 
-def normalize(images, cross_gram):
-    factor = jnp.linalg.cholesky(cross_gram)
-    return lax.linalg.triangular_solve(
-        factor, images, left_side=False, lower=True, transpose_a=True
-    )
-
-
-def refine_whole(gram_full, initial):
-    vectors = initial
-    for sweep_index in range(ITERS):
-        images = jnp.dot(gram_full, vectors, precision=precise)
-        vectors = normalize(images, jnp.dot(images.T, images, precision=precise))
-    return vectors
-
-
-def whole(blocks, scale):
-    b = {}
+def dot(a, b, dims=((1,), (0,))):
+    return lax.dot_general(a, b, (dims, ((), ())), precision=precise, preferred_element_type=jnp.float32)
+
+
+def inverse_factor(c):
+    lane = lax.broadcasted_iota(jnp.int32, (8, 128), 1)
+    row = lax.broadcasted_iota(jnp.int32, (8, 128), 0)
+    tiles = [c[8 * i : 8 * (i + 1)] for i in range(RANK // 8)]
+    result = []
+
+    def spread_lane(tile, n):
+        return jnp.broadcast_to(tile[:, n : n + 1], (8, 128))
+
+    def spread_row(tile, n):
+        return jnp.broadcast_to(tile[n : n + 1, :], (8, 128))
+
+    for k in range(RANK // 8):
+        lo = 8 * k
+        inside = (lane >= lo) & (lane < lo + 8)
+        columns = [[spread_lane(tiles[i], lo + t) for t in range(8)] for i in range(k, RANK // 8)]
+        d = [[spread_row(columns[0][t], s) for t in range(s + 1)] for s in range(8)]
+        unit = jnp.where(inside, jnp.where(lane - lo == row, 1.0, 0.0), tiles[k])
+        p = [spread_row(unit, s) for s in range(8)]
+        rd = [None] * 8
+        m = [[None] * 8 for _ in range(8)]
+        for t in range(8):
+            rd[t] = 1.0 / d[t][t]
+            for s in range(t + 1, 8):
+                m[s][t] = d[s][t] * rd[t]
+                for u in range(t + 1, s + 1):
+                    d[s][u] = d[s][u] - m[s][t] * d[u][t]
+                p[s] = p[s] - m[s][t] * p[t]
+        rows = p[0] * lax.rsqrt(d[0][0])
+        for s in range(1, 8):
+            rows = jnp.where(row == s, p[s] * lax.rsqrt(d[s][s]), rows)
+        result.append(jnp.where(lane < lo + 8, rows, 0.0))
+        if k + 1 == RANK // 8:
+            break
+        q = [p[t] * rd[t] for t in range(8)]
+        for s in range(7, 0, -1):
+            for t in range(s):
+                q[t] = q[t] - m[s][t] * q[s]
+        for i in range(k + 1, RANK // 8):
+            col = columns[i - k]
+            new = jnp.where(inside, 0.0, tiles[i])
+            for t in range(8):
+                new = new - col[t] * q[t]
+            tiles[i] = new
+    return jnp.concatenate(result, axis=0)
+
+
+def refine_kernel(scale, blocks_ref, start_ref, out_ref, g_ref):
     for n, (p, q) in enumerate(BLOCKS):
-        block = blocks[128 * n : 128 * (n + 1)] * scale
-        b[p, q] = block
+        block = blocks_ref[128 * n : 128 * (n + 1)] * scale
+        g_ref[128 * p : 128 * (p + 1), 128 * q : 128 * (q + 1)] = block
         if p != q:
-            b[q, p] = block.T
-    return jnp.concatenate([jnp.concatenate([b[p, q] for q in range(4)], axis=1) for p in range(4)], axis=0)
+            g_ref[128 * q : 128 * (q + 1), 128 * p : 128 * (p + 1)] = block.T
+    pad = jnp.zeros((128 - RANK, 512), jnp.float32)
+
+    def factor(images):
+        full = jnp.concatenate([images, pad], axis=0)
+        return inverse_factor(dot(images, full, ((1,), (1,))))
+
+    def sweep(_, images):
+        ahead = dot(images, g_ref[...])
+        return dot(factor(images), jnp.concatenate([ahead, pad], axis=0))
+
+    images = dot(start_ref[...], g_ref[...])
+    images = lax.fori_loop(0, ITERS - 1, sweep, images)
+    out_ref[...] = dot(factor(images), jnp.concatenate([images, pad], axis=0))
+
+
+def refine(blocks, start_t, scale, name):
+    vmem = pl.BlockSpec(memory_space=pltpu.VMEM)
+    return pl.pallas_call(
+        functools.partial(refine_kernel, scale),
+        out_shape=jax.ShapeDtypeStruct((RANK, 512), jnp.float32),
+        in_specs=[vmem] * 2,
+        out_specs=vmem,
+        scratch_shapes=[pltpu.VMEM((512, 512), jnp.float32)],
+        compiler_params=pltpu.CompilerParams(vmem_limit_bytes=32 * 1024 * 1024),
+        name=name,
+    )(blocks, start_t)
 
 
 def body(snapshot, start_one, start_two):
     fibers, blocks = exchange(first_kernel, "first", 0, [(I1, COLS), (GROWS, 128)], FIRST)(snapshot)
-    basis_one = refine_whole(whole(blocks, 1.0 / (I2 * COLS)), start_one)
-    fibers_two, blocks = exchange(second_kernel, "second", 1, [(I2, 128), (GROWS, 128)], SECOND)(basis_one.T, fibers)
-    basis_two = refine_whole(whole(blocks, 1.0 / (RANK * COLS)), start_two)
-    core_tensor = exchange(third_kernel, "third", 2, [(6, 3, COLS)], THIRD)(basis_two.T, fibers_two)
-    return (basis_one, basis_two, core_tensor)
+    basis_one = refine(blocks, start_one.T, 1.0 / (I2 * COLS), "refine_one")
+    fibers_two, blocks = exchange(second_kernel, "second", 1, [(I2, 128), (GROWS, 128)], SECOND)(basis_one, fibers)
+    basis_two = refine(blocks, start_two.T, 1.0 / (RANK * COLS), "refine_two")
+    core_tensor = exchange(third_kernel, "third", 2, [(6, 3, COLS)], THIRD)(basis_two, fibers_two)
+    return (basis_one.T, basis_two.T, core_tensor)
 
 
 def solution(mesh):

time: 401 us -> 221 us (0.55)
  other arithmetic: 211 us -> 0 us
  Pallas kernels: 157 us -> 216 us
  matrix products: 22.5 us -> 0 us
    another operation x60 -> x0, other arithmetic: 210 us -> none  [the longest x36 114 us: normalize(): factor = jnp.linalg.cholesky(cross_gram)]
    pallas_call x0 -> x2, Pallas kernels: none -> 58.7 us  [refine(): pl.pallas_call(functools.partial(refine_kernel, scale), out_shape=jax.Sha...]
    dot_general x24 -> x0, matrix products: 18.1 us -> none  [the longest x12 13.8 us: refine_whole(): images = jnp.dot(gram_full, vectors, precision=precise)]
    another operation x12 -> x0, matrix products: 4.46 us -> none  [normalize(): lax.linalg.triangular_solve(factor, images, left_side=False, lower=True,...]
where the time goes in v2:
time: 221 us
  Pallas kernels  216 us (98%)
  local copies, waits for them, and re-layouts  3.61 us (2%)
    pallas_call x3, Pallas kernels, call(): pl.pallas_call(body, out_shape=shapes[0] if single else shapes, in_specs=...  158 us
    pallas_call x2, Pallas kernels, refine(): pl.pallas_call(functools.partial(refine_kernel, scale), out_shape=jax.Sha...  58.7 us

profile of v2, /device:TPU:1, one launch (start us, length us, event | category | flops | bytes accessed | tf_op | source)
XLA Modules:
  0.0 220.6 jit_solution(140383454741440749)
XLA Ops:
  0.6 0.0 copy-start
  0.6 1.1 copy-done
  1.8 0.0 copy-start.3
  1.8 71.9 %first.1 = (f32[512,384]{1,0:T(8,128)S(1)}, f32[1280,128]{1,0:T(8,128)S(1)}) custom-call(f32[32,16,384]{2,1,0:T(8,128)S(1)} %copy-done), custom_call_target="tpu_custom_call" | custom-call | tf_op jit(solution)/shard_map/first/pallas_call | solution.py:322
  73.6 0.0 copy-done.3
  73.7 29.3 %refine_one.1.refs_0_ = f32[96,512]{1,0:T(8,128)} custom-call(f32[1280,128]{1,0:T(8,128)S(1)} %get-tuple-element.7.blocks_ref, f32[96,512]{1,0:T(8,128)S(1)} %bitcast.6), custom_call_target="tpu_custom_call" | custom-call | tf_op jit(solution)/shard_map/refine_one/pallas_call | solution.py:411
  103.0 0.0 copy-start.2
  103.0 0.9 copy-done.2
  103.9 0.0 copy-start.4
  103.9 66.0 %second.1 = (f32[512,128]{1,0:T(8,128)S(1)}, f32[1280,128]{1,0:T(8,128)S(1)}) custom-call(f32[96,512]{1,0:T(8,128)S(1)} %copy-done.2, f32[512,384]{1,0:T(8,128)S(1)} %get-tuple-element.8.refs_1_), custom_call_target="tpu_custom_call" | custom-call | tf_op jit(solution)/shard_map/second/pallas_call | solution.py:322
  169.9 0.0 copy-done.4
  169.9 29.3 %refine_two.1.refs_0_ = f32[96,512]{1,0:T(8,128)} custom-call(f32[1280,128]{1,0:T(8,128)S(1)} %get-tuple-element.9.blocks_ref, f32[96,512]{1,0:T(8,128)S(1)} %bitcast.7), custom_call_target="tpu_custom_call" | custom-call | tf_op jit(solution)/shard_map/refine_two/pallas_call | solution.py:411
  199.3 0.0 copy-start.1
  199.3 0.9 copy-done.1
  200.2 19.8 %third.1 = f32[6,3,384]{2,1,0:T(4,128)S(1)} custom-call(f32[96,512]{1,0:T(8,128)S(1)} %copy-done.1, f32[512,128]{1,0:T(8,128)S(1)} %get-tuple-element.10.refs_1_), custom_call_target="tpu_custom_call" | custom-call | tf_op jit(solution)/shard_map/third/pallas_call | solution.py:322
  220.0 0.6 copy.7
Async XLA Ops:
  0.6 1.1 copy-start
  1.8 71.9 %copy-start.3 = (f32[512,96]{0,1:T(8,128)S(1)}, f32[512,96]{0,1:T(8,128)}, u32[]{:S(2)}) copy-start(f32[512,96]{0,1:T(8,128)} %param.4) | copy-start | bytes 589828
  103.0 0.9 copy-start.2
  103.9 66.0 %copy-start.4 = (f32[512,96]{0,1:T(8,128)S(1)}, f32[512,96]{0,1:T(8,128)}, u32[]{:S(2)}) copy-start(f32[512,96]{0,1:T(8,128)} %param.5) | copy-start | bytes 589828
  199.3 0.9 copy-start.1

commit v3 on v2

v3 whole, which is shorter than its diff:
```python
import functools

import jax
import jax.numpy as jnp
from jax import lax
from jax.experimental import pallas as pl
from jax.experimental.pallas import tpu as pltpu
from jax.sharding import PartitionSpec as P

I1 = 512
I2 = 512
COLS = 384
RANK = 96
ITERS = 6
GX = 16
GY = 32
NX = 4
NY = 4
BLOCKS = [(p, q) for p in range(4) for q in range(p, 4)]
GROWS = 128 * len(BLOCKS)
HALF = GROWS // 2
PIECE = HALF // 16
QUARTER = PIECE // 4

MESH = pl.DeviceIdType.MESH
precise = lax.Precision.HIGHEST


def place():
    gx = lax.axis_index("gx")
    gy = lax.axis_index("gy")
    x, z_lo = lax.div(gx, 4), lax.rem(gx, 4)
    z_hi = lax.div(gy, 8)
    y = lax.rem(lax.div(gy, 2), 4)
    core = lax.rem(gy, 2)
    return gx, gy, x, y, z_hi, z_lo, core


def remote(src, dst, send, recv, target):
    return pltpu.make_async_remote_copy(
        src_ref=src, dst_ref=dst, send_sem=send, recv_sem=recv, device_id=target, device_id_type=MESH
    )


def gx_peer(d):
    gx, gy = place()[:2]
    return (lax.rem(gx + d, GX), gy)


def gy_peer(d):
    gx, gy = place()[:2]
    return (gx, lax.bitwise_xor(gy, d))


def sibling():
    gx, gy, *_, core = place()
    return (gx, gy + 1 - 2 * core)


def xy_peer(dx, dy):
    gx, gy, x, y, z_hi, z_lo, core = place()
    px, py = lax.rem(x + dx, NX), lax.rem(y + dy, NY)
    return (px * 4 + z_lo, z_hi * 8 + py * 2 + core), px * 4 + py


def z_lo_peer(d):
    gx, gy, x, y, z_hi, z_lo, core = place()
    other = lax.rem(z_lo + d, 4)
    return (x * 4 + other, gy), other


def z_hi_peer(d):
    gx, gy, x, y, z_hi, z_lo, core = place()
    return (gx, lax.rem(z_hi + d, 4) * 8 + y * 2 + core)


def meet(peers):
    barrier = pltpu.get_barrier_semaphore()
    for peer in peers:
        pl.semaphore_signal(barrier, inc=1, device_id=peer, device_id_type=MESH)
    pl.semaphore_wait(barrier, len(peers))


XY = [(dx, dy) for dx in range(NX) for dy in range(NY) if (dx, dy) != (0, 0)]


def all_reduce(gp, total, s):
    gx, gy, x, y, z_hi, z_lo, core = place()
    mine = pl.multiple_of(core * HALF, 8)
    other = pl.multiple_of((1 - core) * HALF, 8)
    done = []
    copy = remote(gp.at[pl.ds(other, HALF)], s["rc"], s["c1s"], s["c1r"], sibling())
    copy.start()
    copy.wait_recv()
    done.append(copy)
    s["h"][...] = gp[pl.ds(mine, HALF)] + s["rc"][...]
    copies = []
    for o, (dx, dy) in enumerate(XY):
        peer, q = xy_peer(dx, dy)
        copy = remote(
            s["h"].at[pl.ds(pl.multiple_of(q * PIECE, 8), PIECE)],
            s["rxy"].at[o], s["x1s"].at[o], s["x1r"].at[o], peer,
        )
        copy.start()
        copies.append(copy)
    me = x * 4 + y
    acc = s["h"][pl.ds(pl.multiple_of(me * PIECE, 8), PIECE)]
    for o, copy in enumerate(copies):
        copy.wait_recv()
        acc = acc + s["rxy"][o]
    done += copies
    for i in range(4):
        s["za"][i] = acc[QUARTER * i : QUARTER * (i + 1)]
    copies = []
    for d in range(1, 4):
        peer, other = z_lo_peer(d)
        copy = remote(s["za"].at[other], s["rzl"].at[d - 1], s["z1s"].at[d - 1], s["z1r"].at[d - 1], peer)
        copy.start()
        copies.append(copy)
    part = s["za"][z_lo]
    for d, copy in enumerate(copies):
        copy.wait_recv()
        part = part + s["rzl"][d]
    done += copies
    s["zh"][z_hi] = part
    copies = []
    for d in range(1, 4):
        copy = remote(s["zh"].at[z_hi], s["zh"].at[z_hi], s["z2s"].at[d - 1], s["z2r"].at[d - 1], z_hi_peer(d))
        copy.start()
        copies.append(copy)
    for copy in copies:
        copy.wait_recv()
    done += copies
    s["zl"][z_lo] = (s["zh"][0] + s["zh"][1]) + (s["zh"][2] + s["zh"][3])
    copies = []
    for d in range(1, 4):
        peer, _ = z_lo_peer(d)
        copy = remote(s["zl"].at[z_lo], s["zl"].at[z_lo], s["z3s"].at[d - 1], s["z3r"].at[d - 1], peer)
        copy.start()
        copies.append(copy)
    for copy in copies:
        copy.wait_recv()
    done += copies
    s["agz"][...] = jnp.concatenate([s["zl"][i] for i in range(4)], axis=0)
    own = pl.ds(pl.multiple_of(mine + me * PIECE, 8), PIECE)
    copies = []
    for o, (dx, dy) in enumerate(XY):
        peer, q = xy_peer(dx, dy)
        copy = remote(s["agz"], total.at[own], s["x2s"].at[o], s["x2r"].at[o], peer)
        copy.start()
        copies.append(copy)
    total[own] = s["agz"][...]
    for copy in copies:
        copy.wait_recv()
    done += copies
    copy = remote(total.at[pl.ds(mine, HALF)], total.at[pl.ds(mine, HALF)], s["c2s"], s["c2r"], sibling())
    copy.start()
    copy.wait_recv()
    done.append(copy)
    for copy in done:
        copy.wait_send()


DMA = pltpu.SemaphoreType.DMA
REDUCE = dict(
    gp=pltpu.VMEM((GROWS, 128), jnp.float32),
    total=pltpu.VMEM((GROWS, 128), jnp.float32),
    rc=pltpu.VMEM((HALF, 128), jnp.float32),
    h=pltpu.VMEM((HALF, 128), jnp.float32),
    rxy=pltpu.VMEM((15, PIECE, 128), jnp.float32),
    za=pltpu.VMEM((4, QUARTER, 128), jnp.float32),
    rzl=pltpu.VMEM((3, QUARTER, 128), jnp.float32),
    zh=pltpu.VMEM((4, QUARTER, 128), jnp.float32),
    zl=pltpu.VMEM((4, QUARTER, 128), jnp.float32),
    agz=pltpu.VMEM((PIECE, 128), jnp.float32),
    c1s=DMA, c1r=DMA, c2s=DMA, c2r=DMA,
    x1s=DMA((15,)), x1r=DMA((15,)), x2s=DMA((15,)), x2r=DMA((15,)),
    z1s=DMA((3,)), z1r=DMA((3,)), z2s=DMA((3,)), z2r=DMA((3,)), z3s=DMA((3,)), z3r=DMA((3,)),
)


def gram_blocks(flat, gp):
    n = 0
    for p in range(4):
        strip = lax.dot_general(
            flat[128 * p : 128 * (p + 1)], flat[128 * p :], (((1,), (1,)), ((), ())),
            precision=precise, preferred_element_type=jnp.float32,
        )
        for q in range(4 - p):
            gp[128 * n : 128 * (n + 1)] = strip[:, 128 * q : 128 * (q + 1)]
            n += 1


def swap_granules(tiles):
    lane = lax.broadcasted_iota(jnp.int32, tiles[0].shape, 1)
    tiles = list(tiles)
    for bit in range(4):
        shift = 8 << bit
        low = lax.bitwise_and(lane, shift) == 0
        for j in range(16):
            if not j >> bit & 1:
                k = j | 1 << bit
                a, b = tiles[j], tiles[k]
                tiles[j] = jnp.where(low, a, pltpu.roll(b, shift, 1))
                tiles[k] = jnp.where(low, pltpu.roll(a, 128 - shift, 1), b)
    return tiles


def plane_peers():
    return [xy_peer(dx, dy)[0] for dx in range(1, NX) for dy in range(1, NY)]


def gather_one(x_ref, s):
    gx, gy, *_ = place()
    copies = []
    for half in range(2):
        for i in range(2 * half, 2 * half + 2):
            rows = slice(8 * i, 8 * (i + 1))
            for c in range(3):
                lanes = slice(128 * c, 128 * (c + 1))
                for g, tile in enumerate(swap_granules([x_ref[rows, j, lanes] for j in range(16)])):
                    s["xs"][g, rows, lanes] = tile
        rows = pl.ds(16 * half, 16)
        for d in range(1, GX):
            peer = gx_peer(d)
            copy = remote(
                s["xs"].at[peer[0], rows], s["fib"].at[gx, rows],
                s["as"].at[half, d - 1], s["ar"].at[half, d - 1], peer,
            )
            copy.start()
            copies.append(copy)
    s["fib"][gx] = s["xs"][gx]
    for copy in copies:
        copy.wait_recv()
    return copies


def gather_two(basis, fibers, s):
    gx, gy, *_ = place()
    shrunk = dot(basis, fibers)
    for u in range(GY):
        s["st"][u] = shrunk[3 * u : 3 * (u + 1)]
    copies = []
    for d in range(1, GY):
        peer = gy_peer(d)
        copy = remote(s["st"].at[peer[1]], s["f2"].at[gy], s["bs"].at[d - 1], s["br"].at[d - 1], peer)
        copy.start()
        copies.append(copy)
    s["f2"][gy] = s["st"][gy]
    for copy in copies:
        copy.wait_recv()
    tiles = [s["f2"][:, a, 128 * c : 128 * (c + 1)] for a in range(3) for c in range(3)]
    tiles += [jnp.zeros((GY, 128), jnp.float32)] * 7
    return jnp.concatenate(swap_granules(tiles), axis=0), copies


def spread_core(basis, columns, out_ref, s):
    gx, gy, *_ = place()
    row, half = lax.div(gy, 2), lax.rem(gy, 2)
    core = dot(basis, columns)
    for u in range(GY):
        s["cs"][u] = core[3 * u : 3 * (u + 1)]

    def copy(d):
        u = lax.bitwise_xor(gy, d)
        return remote(s["cs"].at[u], s["ro"].at[gx, half], s["ks"].at[d], s["kr"].at[gx, half], (row, u))

    @pl.when(row != gx)
    def _():
        copy(0).start()

    @pl.when(row == gx)
    def _():
        s["ro"][gx, half] = s["cs"][gy]

    for d in range(1, GY):
        copy(d).start()

    def arrival(k, h):
        source = lax.rem(gx + k, GX)
        return remote(s["cs"].at[0], s["ro"].at[source, h], s["ks"].at[0], s["kr"].at[source, h], (source, 2 * gx + h))

    for h in range(2):
        @pl.when(2 * gx + h != gy)
        def _(h=h):
            arrival(0, h).wait_recv()
        for k in range(1, GX):
            arrival(k, h).wait_recv()
    for h in range(2):
        tiles = swap_granules([s["ro"][g, h] for g in range(GX)])
        for a in range(3):
            for c in range(3):
                out_ref[3 * h + a, :, 128 * c : 128 * (c + 1)] = tiles[3 * a + c]

    @pl.when(row != gx)
    def _():
        copy(0).wait_send()

    for d in range(1, GY):
        copy(d).wait_send()


def first_kernel(x_ref, fib_ref, g_ref, s):
    meet([gx_peer(d) for d in range(1, GX)] + [gy_peer(d) for d in range(1, GY)] + plane_peers())
    copies = gather_one(x_ref, s)
    flat = s["fib"][...].reshape(I1, COLS)
    fib_ref[...] = flat
    gram_blocks(flat, s["gp"])
    all_reduce(s["gp"], s["total"], s)
    g_ref[...] = s["total"][...]
    for copy in copies:
        copy.wait_send()


def second_kernel(basis_ref, fib_ref, f2_ref, g_ref, s):
    meet([gx_peer(d) for d in range(1, GX)] + [gy_peer(d) for d in range(1, GY)] + plane_peers())
    flat, copies = gather_two(basis_ref[...], fib_ref[...], s)
    f2_ref[...] = flat
    gram_blocks(flat, s["gp"])
    all_reduce(s["gp"], s["total"], s)
    g_ref[...] = s["total"][...]
    for copy in copies:
        copy.wait_send()


def third_kernel(basis_ref, f2_ref, out_ref, s):
    gx, gy, *_ = place()
    barrier = pltpu.get_barrier_semaphore()
    for h in range(2):
        @pl.when(2 * gx + h != gy)
        def _(h=h):
            pl.semaphore_signal(barrier, inc=1, device_id=(gx, 2 * gx + h), device_id_type=MESH)
        for k in range(1, GX):
            pl.semaphore_signal(barrier, inc=1, device_id=(lax.rem(gx + k, GX), 2 * gx + h), device_id_type=MESH)

    @pl.when(lax.div(gy, 2) == gx)
    def _():
        pl.semaphore_wait(barrier, 31)

    @pl.when(lax.div(gy, 2) != gx)
    def _():
        pl.semaphore_wait(barrier, 32)

    spread_core(basis_ref[...], f2_ref[...], out_ref, s)


FIRST = REDUCE | dict(
    xs=pltpu.VMEM((GX, 32, COLS), jnp.float32), fib=pltpu.VMEM((GX, 32, COLS), jnp.float32),
    **{"as": DMA((2, 15)), "ar": DMA((2, 15))},
)
SECOND = REDUCE | dict(
    st=pltpu.VMEM((GY, 3, COLS), jnp.float32), f2=pltpu.VMEM((GY, 3, COLS), jnp.float32),
    bs=DMA((31,)), br=DMA((31,)),
)
THIRD = dict(
    cs=pltpu.VMEM((GY, 3, 128), jnp.float32), ro=pltpu.VMEM((GX, 2, 3, 128), jnp.float32),
    ks=DMA((32,)), kr=DMA((GX, 2)),
)

VMEM = pl.BlockSpec(memory_space=pltpu.VMEM)


def exchange(kernel, name, ident, outs, scratch):
    def body(*refs):
        count = len(refs) - 1
        kernel(*refs[:count], refs[count])

    def call(*args):
        single = len(outs) == 1
        shapes = [jax.ShapeDtypeStruct(o, jnp.float32) for o in outs]
        return pl.pallas_call(
            body,
            out_shape=shapes[0] if single else shapes,
            in_specs=[VMEM] * len(args),
            out_specs=VMEM if single else [VMEM] * len(outs),
            scratch_shapes=[scratch],
            compiler_params=pltpu.CompilerParams(
                collective_id=ident, has_side_effects=True, vmem_limit_bytes=32 * 1024 * 1024
            ),
            name=name,
        )(*args)

    return call


def dot(a, b, dims=((1,), (0,))):
    return lax.dot_general(a, b, (dims, ((), ())), precision=precise, preferred_element_type=jnp.float32)


def inverse_factor(c):
    lane = lax.broadcasted_iota(jnp.int32, (8, 128), 1)
    row = lax.broadcasted_iota(jnp.int32, (8, 128), 0)
    tiles = [c[8 * i : 8 * (i + 1)] for i in range(RANK // 8)]
    result = []

    def spread_lane(tile, n):
        return jnp.broadcast_to(tile[:, n : n + 1], (8, 128))

    def spread_row(tile, n):
        return jnp.broadcast_to(tile[n : n + 1, :], (8, 128))

    for k in range(RANK // 8):
        lo = 8 * k
        inside = (lane >= lo) & (lane < lo + 8)
        columns = [[spread_lane(tiles[i], lo + t) for t in range(8)] for i in range(k, min(k + 2 + 1, RANK // 8))]
        d = [[spread_row(columns[0][t], s) for t in range(s + 1)] for s in range(8)]
        unit = jnp.where(inside, jnp.where(lane - lo == row, 1.0, 0.0), tiles[k])
        p = [spread_row(unit, s) for s in range(8)]
        rd = [None] * 8
        m = [[None] * 8 for _ in range(8)]
        for t in range(8):
            rd[t] = 1.0 / d[t][t]
            for s in range(t + 1, 8):
                m[s][t] = d[s][t] * rd[t]
                for u in range(t + 1, s + 1):
                    d[s][u] = d[s][u] - m[s][t] * d[u][t]
                p[s] = p[s] - m[s][t] * p[t]
        rows = p[0] * lax.rsqrt(d[0][0])
        for s in range(1, 8):
            rows = jnp.where(row == s, p[s] * lax.rsqrt(d[s][s]), rows)
        result.append(jnp.where(lane < lo + 8, rows, 0.0))
        if k + 1 == RANK // 8:
            break
        q = [p[t] * rd[t] for t in range(8)]
        for s in range(7, 0, -1):
            for t in range(s):
                q[t] = q[t] - m[s][t] * q[s]
        near = min(k + 2, RANK // 8 - 1)
        if near + 1 < RANK // 8:
            picked = q[0]
            for t in range(1, 8):
                picked = jnp.where(row == t, q[t], picked)
            spread = [picked] if k == 0 else [jnp.zeros((lo, 128), jnp.float32), picked]
            spread = jnp.concatenate(spread + [jnp.zeros((120 - lo, 128), jnp.float32)], axis=0)
            far = jnp.concatenate(tiles[near + 1 :], axis=0)
            change = dot(far, spread)
        for i in range(k + 1, RANK // 8):
            new = jnp.where(inside, 0.0, tiles[i])
            if i <= near:
                col = columns[i - k]
                for t in range(8):
                    new = new - col[t] * q[t]
            else:
                at = 8 * (i - near - 1)
                new = new - change[at : at + 8]
            tiles[i] = new
    return jnp.concatenate(result, axis=0)


def refine_kernel(scale, blocks_ref, start_ref, out_ref, g_ref):
    for n, (p, q) in enumerate(BLOCKS):
        block = blocks_ref[128 * n : 128 * (n + 1)] * scale
        g_ref[128 * p : 128 * (p + 1), 128 * q : 128 * (q + 1)] = block
        if p != q:
            g_ref[128 * q : 128 * (q + 1), 128 * p : 128 * (p + 1)] = block.T
    pad = jnp.zeros((128 - RANK, 512), jnp.float32)

    def factor(images):
        full = jnp.concatenate([images, pad], axis=0)
        return inverse_factor(dot(images, full, ((1,), (1,))))

    def sweep(_, images):
        ahead = dot(images, g_ref[...])
        return dot(factor(images), jnp.concatenate([ahead, pad], axis=0))

    images = dot(start_ref[...], g_ref[...])
    images = lax.fori_loop(0, ITERS - 1, sweep, images)
    out_ref[...] = dot(factor(images), jnp.concatenate([images, pad], axis=0))


def refine(blocks, start_t, scale, name):
    vmem = pl.BlockSpec(memory_space=pltpu.VMEM)
    return pl.pallas_call(
        functools.partial(refine_kernel, scale),
        out_shape=jax.ShapeDtypeStruct((RANK, 512), jnp.float32),
        in_specs=[vmem] * 2,
        out_specs=vmem,
        scratch_shapes=[pltpu.VMEM((512, 512), jnp.float32)],
        compiler_params=pltpu.CompilerParams(vmem_limit_bytes=32 * 1024 * 1024),
        name=name,
    )(blocks, start_t)


def body(snapshot, start_one, start_two):
    start_two = start_two.reshape(GY, 16, RANK).transpose(2, 1, 0).reshape(RANK, I2)
    fibers, blocks = exchange(first_kernel, "first", 0, [(I1, COLS), (GROWS, 128)], FIRST)(snapshot)
    basis_one = refine(blocks, start_one.T, 1.0 / (I2 * COLS), "refine_one")
    fibers_two, blocks = exchange(second_kernel, "second", 1, [(I2, 128), (GROWS, 128)], SECOND)(basis_one, fibers)
    basis_two = refine(blocks, start_two, 1.0 / (RANK * COLS), "refine_two")
    core_tensor = exchange(third_kernel, "third", 2, [(6, 3, COLS)], THIRD)(basis_two, fibers_two)
    basis_two = basis_two.reshape(RANK, 16, GY).transpose(2, 1, 0).reshape(I2, RANK)
    return (basis_one.T, basis_two, core_tensor)


def solution(mesh):
    in_specs = (P("gx", "gy", None), P(), P())
    out_specs = (P(), P(), P("gx", "gy", None))
    return jax.shard_map(body, mesh=mesh, in_specs=in_specs, out_specs=out_specs, check_vma=False)
```

time: 221 us -> 196 us (0.89)
  the two profiles are of different devices: /device:TPU:1 before, /device:TPU:5 now
where the time goes in v3:
time: 196 us
  Pallas kernels  191 us (97%)
  local copies, waits for them, and re-layouts  4.09 us (2%)
    pallas_call x3, Pallas kernels, call(): pl.pallas_call(body, out_shape=shapes[0] if single else shapes, in_specs=...  145 us
    pallas_call x2, Pallas kernels, refine(): pl.pallas_call(functools.partial(refine_kernel, scale), out_shape=jax.Sha...  46.7 us

profile of v3, /device:TPU:5, one launch (start us, length us, event | category | flops | bytes accessed | tf_op | source)
XLA Modules:
  0.0 196.0 jit_solution(11838238156944979261)
XLA Ops:
  0.6 0.0 copy-start
  0.6 1.1 copy-done
  1.8 0.0 copy-start.2
  1.8 68.2 %first.1 = (f32[512,384]{1,0:T(8,128)S(1)}, f32[1280,128]{1,0:T(8,128)S(1)}) custom-call(f32[32,16,384]{2,1,0:T(8,128)S(1)} %copy-done), custom_call_target="tpu_custom_call" | custom-call | tf_op jit(solution)/shard_map/first/pallas_call | solution.py:371
  69.9 0.0 copy-done.2
  69.9 23.7 %refine_one.1.refs_0_ = f32[96,512]{1,0:T(8,128)} custom-call(f32[1280,128]{1,0:T(8,128)S(1)} %get-tuple-element.7.blocks_ref, f32[96,512]{1,0:T(8,128)S(1)} %bitcast.11), custom_call_target="tpu_custom_call" | custom-call | tf_op jit(solution)/shard_map/refine_one/pallas_call | solution.py:473
  93.6 0.0 copy-start.1
  93.6 0.9 copy-done.1
  94.5 0.0 copy-start.3
  94.5 58.6 %second.1 = (f32[512,128]{1,0:T(8,128)S(1)}, f32[1280,128]{1,0:T(8,128)S(1)}) custom-call(f32[96,512]{1,0:T(8,128)S(1)} %copy-done.1, f32[512,384]{1,0:T(8,128)S(1)} %get-tuple-element.8.refs_1_), custom_call_target="tpu_custom_call" | custom-call | tf_op jit(solution)/shard_map/second/pallas_call | solution.py:371
  153.1 0.0 copy-done.3
  153.1 0.1 copy.8
  153.3 0.1 copy.9
  153.4 0.1 copy.10.start_ref
  153.5 23.0 %refine_two.1.refs_0_ = f32[96,512]{1,0:T(8,128)S(1)} custom-call(f32[1280,128]{1,0:T(8,128)S(1)} %get-tuple-element.9.blocks_ref, f32[96,512]{1,0:T(8,128)S(1)} %copy.10.start_ref), custom_call_target="tpu_custom_call" | custom-call | tf_op jit(solution)/shard_map/refine_two/pallas_call | solution.py:473
  176.5 17.8 %third.1 = f32[6,3,384]{2,1,0:T(4,128)S(1)} custom-call(f32[96,512]{1,0:T(8,128)S(1)} %refine_two.1.refs_0_, f32[512,128]{1,0:T(8,128)S(1)} %get-tuple-element.10.refs_1_), custom_call_target="tpu_custom_call" | custom-call | tf_op jit(solution)/shard_map/third/pallas_call | solution.py:371
  194.3 0.1 copy.11
  194.4 0.2 copy.12
  194.6 0.8 copy.13
  195.4 0.6 copy.15
Async XLA Ops:
  0.6 1.1 copy-start
  1.8 68.2 %copy-start.2 = (f32[512,96]{0,1:T(8,128)S(1)}, f32[512,96]{0,1:T(8,128)}, u32[]{:S(2)}) copy-start(f32[512,96]{0,1:T(8,128)} %param.4) | copy-start | bytes 589828
  93.6 0.9 copy-start.1
  94.5 58.6 %copy-start.3 = (f32[512,96]{0,1:T(8,128)S(1)}, f32[512,96]{0,1:T(8,128)}, u32[]{:S(2)}) copy-start(f32[512,96]{0,1:T(8,128)} %param.5) | copy-start | bytes 589828

commit v4 on v3

--- a/solution.py
+++ b/solution.py
@@ -74,11 +74,14 @@
     return (gx, lax.rem(z_hi + d, 4) * 8 + y * 2 + core)
 
 
-def meet(peers):
+def greet(peers):
     barrier = pltpu.get_barrier_semaphore()
     for peer in peers:
         pl.semaphore_signal(barrier, inc=1, device_id=peer, device_id_type=MESH)
-    pl.semaphore_wait(barrier, len(peers))
+
+
+def await_greetings(count):
+    pl.semaphore_wait(pltpu.get_barrier_semaphore(), count)
 
 
 XY = [(dx, dy) for dx in range(NX) for dy in range(NY) if (dx, dy) != (0, 0)]
@@ -210,16 +213,26 @@
     return [xy_peer(dx, dy)[0] for dx in range(1, NX) for dy in range(1, NY)]
 
 
+def everyone():
+    return [gx_peer(d) for d in range(1, GX)] + [gy_peer(d) for d in range(1, GY)] + plane_peers()
+
+
 def gather_one(x_ref, s):
     gx, gy, *_ = place()
+    load = pltpu.make_async_copy(x_ref, s["x"], s["xc"])
+    load.start()
+    peers = everyone()
+    greet(peers)
+    load.wait()
     copies = []
     for half in range(2):
-        for i in range(2 * half, 2 * half + 2):
-            rows = slice(8 * i, 8 * (i + 1))
-            for c in range(3):
-                lanes = slice(128 * c, 128 * (c + 1))
-                for g, tile in enumerate(swap_granules([x_ref[rows, j, lanes] for j in range(16)])):
-                    s["xs"][g, rows, lanes] = tile
+        rows = slice(16 * half, 16 * half + 16)
+        for c in range(3):
+            lanes = slice(128 * c, 128 * (c + 1))
+            for g, tile in enumerate(swap_granules([s["x"][rows, j, lanes] for j in range(16)])):
+                s["xs"][g, rows, lanes] = tile
+        if half == 0:
+            await_greetings(len(peers))
         rows = pl.ds(16 * half, 16)
         for d in range(1, GX):
             peer = gx_peer(d)
@@ -235,11 +248,17 @@
     return copies
 
 
-def gather_two(basis, fibers, s):
+def gather_two(basis_ref, fib_ref, s):
     gx, gy, *_ = place()
-    shrunk = dot(basis, fibers)
+    load = pltpu.make_async_copy(fib_ref, s["fib"], s["xc"])
+    load.start()
+    peers = everyone()
+    greet(peers)
+    load.wait()
+    shrunk = dot(basis_ref[...], s["fib"][...])
     for u in range(GY):
         s["st"][u] = shrunk[3 * u : 3 * (u + 1)]
+    await_greetings(len(peers))
     copies = []
     for d in range(1, GY):
         peer = gy_peer(d)
@@ -260,6 +279,7 @@
     core = dot(basis, columns)
     for u in range(GY):
         s["cs"][u] = core[3 * u : 3 * (u + 1)]
+    await_senders()
 
     def copy(d):
         u = lax.bitwise_xor(gy, d)
@@ -301,7 +321,6 @@
 
 
 def first_kernel(x_ref, fib_ref, g_ref, s):
-    meet([gx_peer(d) for d in range(1, GX)] + [gy_peer(d) for d in range(1, GY)] + plane_peers())
     copies = gather_one(x_ref, s)
     flat = s["fib"][...].reshape(I1, COLS)
     fib_ref[...] = flat
@@ -313,8 +332,7 @@
 
 
 def second_kernel(basis_ref, fib_ref, f2_ref, g_ref, s):
-    meet([gx_peer(d) for d in range(1, GX)] + [gy_peer(d) for d in range(1, GY)] + plane_peers())
-    flat, copies = gather_two(basis_ref[...], fib_ref[...], s)
+    flat, copies = gather_two(basis_ref, fib_ref, s)
     f2_ref[...] = flat
     gram_blocks(flat, s["gp"])
     all_reduce(s["gp"], s["total"], s)
@@ -323,7 +341,7 @@
         copy.wait_send()
 
 
-def third_kernel(basis_ref, f2_ref, out_ref, s):
+def greet_senders():
     gx, gy, *_ = place()
     barrier = pltpu.get_barrier_semaphore()
     for h in range(2):
@@ -333,22 +351,31 @@
         for k in range(1, GX):
             pl.semaphore_signal(barrier, inc=1, device_id=(lax.rem(gx + k, GX), 2 * gx + h), device_id_type=MESH)
 
+
+def await_senders():
+    gx, gy, *_ = place()
+
     @pl.when(lax.div(gy, 2) == gx)
     def _():
-        pl.semaphore_wait(barrier, 31)
+        await_greetings(31)
 
     @pl.when(lax.div(gy, 2) != gx)
     def _():
-        pl.semaphore_wait(barrier, 32)
-
+        await_greetings(32)
+
+
+def third_kernel(basis_ref, f2_ref, out_ref, s):
+    greet_senders()
     spread_core(basis_ref[...], f2_ref[...], out_ref, s)
 
 
 FIRST = REDUCE | dict(
+    x=pltpu.VMEM((32, 16, COLS), jnp.float32), xc=DMA,
     xs=pltpu.VMEM((GX, 32, COLS), jnp.float32), fib=pltpu.VMEM((GX, 32, COLS), jnp.float32),
     **{"as": DMA((2, 15)), "ar": DMA((2, 15))},
 )
 SECOND = REDUCE | dict(
+    fib=pltpu.VMEM((I1, COLS), jnp.float32), xc=DMA,
     st=pltpu.VMEM((GY, 3, COLS), jnp.float32), f2=pltpu.VMEM((GY, 3, COLS), jnp.float32),
     bs=DMA((31,)), br=DMA((31,)),
 )
@@ -358,9 +385,10 @@
 )
 
 VMEM = pl.BlockSpec(memory_space=pltpu.VMEM)
-
-
-def exchange(kernel, name, ident, outs, scratch):
+ANY = pl.BlockSpec(memory_space=pl.ANY)
+
+
+def exchange(kernel, name, ident, ins, outs, scratch):
     def body(*refs):
         count = len(refs) - 1
         kernel(*refs[:count], refs[count])
@@ -371,7 +399,7 @@
         return pl.pallas_call(
             body,
             out_shape=shapes[0] if single else shapes,
-            in_specs=[VMEM] * len(args),
+            in_specs=ins,
             out_specs=VMEM if single else [VMEM] * len(outs),
             scratch_shapes=[scratch],
             compiler_params=pltpu.CompilerParams(
@@ -387,7 +415,7 @@
     return lax.dot_general(a, b, (dims, ((), ())), precision=precise, preferred_element_type=jnp.float32)
 
 
-def inverse_factor(c):
+def inverse_factor(c, beside=()):
     lane = lax.broadcasted_iota(jnp.int32, (8, 128), 1)
     row = lax.broadcasted_iota(jnp.int32, (8, 128), 0)
     tiles = [c[8 * i : 8 * (i + 1)] for i in range(RANK // 8)]
@@ -399,13 +427,20 @@
     def spread_row(tile, n):
         return jnp.broadcast_to(tile[n : n + 1, :], (8, 128))
 
+    last = RANK // 8 - 1
+    own = [spread_lane(tiles[0], t) for t in range(8)]
     for k in range(RANK // 8):
         lo = 8 * k
+        near = min(k + 2, last)
         inside = (lane >= lo) & (lane < lo + 8)
-        columns = [[spread_lane(tiles[i], lo + t) for t in range(8)] for i in range(k, min(k + 2 + 1, RANK // 8))]
-        d = [[spread_row(columns[0][t], s) for t in range(s + 1)] for s in range(8)]
+        y = [[spread_lane(tiles[i], lo + t) for t in range(8)] for i in range(k + 1, near + 1)]
+        if k < last:
+            coming = [spread_lane(tiles[k + 1], lo + 8 + t) for t in range(8)]
+        d = [[spread_row(own[t], s) for t in range(s + 1)] for s in range(8)]
         unit = jnp.where(inside, jnp.where(lane - lo == row, 1.0, 0.0), tiles[k])
         p = [spread_row(unit, s) for s in range(8)]
+        if k in (2, 6) and beside:
+            beside[(2, 6).index(k)]()
         rd = [None] * 8
         m = [[None] * 8 for _ in range(8)]
         for t in range(8):
@@ -415,31 +450,35 @@
                 for u in range(t + 1, s + 1):
                     d[s][u] = d[s][u] - m[s][t] * d[u][t]
                 p[s] = p[s] - m[s][t] * p[t]
+                for col in y:
+                    col[s] = col[s] - m[s][t] * col[t]
         rows = p[0] * lax.rsqrt(d[0][0])
         for s in range(1, 8):
             rows = jnp.where(row == s, p[s] * lax.rsqrt(d[s][s]), rows)
         result.append(jnp.where(lane < lo + 8, rows, 0.0))
-        if k + 1 == RANK // 8:
+        if k == last:
             break
-        q = [p[t] * rd[t] for t in range(8)]
-        for s in range(7, 0, -1):
-            for t in range(s):
-                q[t] = q[t] - m[s][t] * q[s]
-        near = min(k + 2, RANK // 8 - 1)
-        if near + 1 < RANK // 8:
+        scaled = [[col[t] * rd[t] for t in range(8)] for col in y]
+        own = list(coming)
+        for u in range(8):
+            for t in range(8):
+                own[u] = own[u] - scaled[0][t] * spread_row(y[0][t], u)
+        if near < last:
+            q = [p[t] * rd[t] for t in range(8)]
+            for s in range(7, 0, -1):
+                for t in range(s):
+                    q[t] = q[t] - m[s][t] * q[s]
             picked = q[0]
             for t in range(1, 8):
                 picked = jnp.where(row == t, q[t], picked)
             spread = [picked] if k == 0 else [jnp.zeros((lo, 128), jnp.float32), picked]
             spread = jnp.concatenate(spread + [jnp.zeros((120 - lo, 128), jnp.float32)], axis=0)
-            far = jnp.concatenate(tiles[near + 1 :], axis=0)
-            change = dot(far, spread)
-        for i in range(k + 1, RANK // 8):
+            change = dot(jnp.concatenate(tiles[near + 1 :], axis=0), spread)
+        for i in range(k + 1, last + 1):
             new = jnp.where(inside, 0.0, tiles[i])
             if i <= near:
-                col = columns[i - k]
                 for t in range(8):
-                    new = new - col[t] * q[t]
+                    new = new - scaled[i - k - 1][t] * p[t]
             else:
                 at = 8 * (i - near - 1)
                 new = new - change[at : at + 8]
@@ -455,13 +494,18 @@
             g_ref[128 * q : 128 * (q + 1), 128 * p : 128 * (p + 1)] = block.T
     pad = jnp.zeros((128 - RANK, 512), jnp.float32)
 
-    def factor(images):
+    def factor(images, beside=()):
         full = jnp.concatenate([images, pad], axis=0)
-        return inverse_factor(dot(images, full, ((1,), (1,))))
+        return inverse_factor(dot(images, full, ((1,), (1,))), beside)
 
     def sweep(_, images):
-        ahead = dot(images, g_ref[...])
-        return dot(factor(images), jnp.concatenate([ahead, pad], axis=0))
+        ahead = []
+
+        def column(n):
+            return lambda: ahead.append(dot(images, g_ref[:, 256 * n : 256 * (n + 1)]))
+
+        inverse = factor(images, [column(n) for n in range(2)])
+        return dot(inverse, jnp.concatenate([jnp.concatenate(ahead, axis=1), pad], axis=0))
 
     images = dot(start_ref[...], g_ref[...])
     images = lax.fori_loop(0, ITERS - 1, sweep, images)
@@ -483,11 +527,11 @@
 
 def body(snapshot, start_one, start_two):
     start_two = start_two.reshape(GY, 16, RANK).transpose(2, 1, 0).reshape(RANK, I2)
-    fibers, blocks = exchange(first_kernel, "first", 0, [(I1, COLS), (GROWS, 128)], FIRST)(snapshot)
+    fibers, blocks = exchange(first_kernel, "first", 0, [ANY], [(I1, COLS), (GROWS, 128)], FIRST)(snapshot)
     basis_one = refine(blocks, start_one.T, 1.0 / (I2 * COLS), "refine_one")
-    fibers_two, blocks = exchange(second_kernel, "second", 1, [(I2, 128), (GROWS, 128)], SECOND)(basis_one, fibers)
+    fibers_two, blocks = exchange(second_kernel, "second", 1, [VMEM, ANY], [(I2, 128), (GROWS, 128)], SECOND)(basis_one, fibers)
     basis_two = refine(blocks, start_two, 1.0 / (RANK * COLS), "refine_two")
-    core_tensor = exchange(third_kernel, "third", 2, [(6, 3, COLS)], THIRD)(basis_two, fibers_two)
+    core_tensor = exchange(third_kernel, "third", 2, [VMEM, VMEM], [(6, 3, COLS)], THIRD)(basis_two, fibers_two)
     basis_two = basis_two.reshape(RANK, 16, GY).transpose(2, 1, 0).reshape(I2, RANK)
     return (basis_one.T, basis_two, core_tensor)
 

time: 196 us -> 187 us (0.954)
  Pallas kernels: 191 us -> 182 us
    pallas_call x2, Pallas kernels: 46.7 us -> 39.2 us  [refine(): pl.pallas_call(functools.partial(refine_kernel, scale), out_shape=jax.Sha...]
where the time goes in v4:
time: 187 us
  Pallas kernels  182 us (97%)
  local copies, waits for them, and re-layouts  4.09 us (2%)
    pallas_call x3, Pallas kernels, call(): pl.pallas_call(body, out_shape=shapes[0] if single else shapes, in_specs=...  143 us
    pallas_call x2, Pallas kernels, refine(): pl.pallas_call(functools.partial(refine_kernel, scale), out_shape=jax.Sha...  39.2 us

profile of v4, /device:TPU:5, one launch (start us, length us, event | category | flops | bytes accessed | tf_op | source)
XLA Modules:
  0.0 186.8 jit_solution(125889685551528796)
XLA Ops:
  0.6 0.0 copy-start
  0.6 1.1 copy-done
  1.8 0.0 copy-start.2
  1.8 67.1 %first.1 = (f32[512,384]{1,0:T(8,128)S(1)}, f32[1280,128]{1,0:T(8,128)S(1)}) custom-call(f32[32,16,384]{2,1,0:T(8,128)S(1)} %copy-done), custom_call_target="tpu_custom_call" | custom-call | tf_op jit(solution)/shard_map/first/pallas_call | solution.py:399
  68.9 0.0 copy-done.2
  68.9 20.0 %refine_one.1.refs_0_ = f32[96,512]{1,0:T(8,128)} custom-call(f32[1280,128]{1,0:T(8,128)S(1)} %get-tuple-element.7.blocks_ref, f32[96,512]{1,0:T(8,128)S(1)} %bitcast.11), custom_call_target="tpu_custom_call" | custom-call | tf_op jit(solution)/shard_map/refine_one/pallas_call | solution.py:517
  88.9 0.0 copy-start.1
  88.9 0.9 copy-done.1
  89.8 0.0 copy-start.3
  89.8 58.2 %second.1 = (f32[512,128]{1,0:T(8,128)S(1)}, f32[1280,128]{1,0:T(8,128)S(1)}) custom-call(f32[96,512]{1,0:T(8,128)S(1)} %copy-done.1, f32[512,384]{1,0:T(8,128)S(1)} %get-tuple-element.8.refs_1_), custom_call_target="tpu_custom_call" | custom-call | tf_op jit(solution)/shard_map/second/pallas_call | solution.py:399
  148.0 0.0 copy-done.3
  148.0 0.1 copy.8
  148.1 0.1 copy.9
  148.2 0.1 copy.10.start_ref
  148.3 19.3 %refine_two.1.refs_0_ = f32[96,512]{1,0:T(8,128)S(1)} custom-call(f32[1280,128]{1,0:T(8,128)S(1)} %get-tuple-element.9.blocks_ref, f32[96,512]{1,0:T(8,128)S(1)} %copy.10.start_ref), custom_call_target="tpu_custom_call" | custom-call | tf_op jit(solution)/shard_map/refine_two/pallas_call | solution.py:517
  167.6 17.5 %third.1 = f32[6,3,384]{2,1,0:T(4,128)S(1)} custom-call(f32[96,512]{1,0:T(8,128)S(1)} %refine_two.1.refs_0_, f32[512,128]{1,0:T(8,128)S(1)} %get-tuple-element.10.refs_1_), custom_call_target="tpu_custom_call" | custom-call | tf_op jit(solution)/shard_map/third/pallas_call | solution.py:399
  185.1 0.1 copy.11
  185.2 0.2 copy.12
  185.4 0.8 copy.13
  186.2 0.6 copy.15
Async XLA Ops:
  0.6 1.1 copy-start
  1.8 67.1 %copy-start.2 = (f32[512,96]{0,1:T(8,128)S(1)}, f32[512,96]{0,1:T(8,128)}, u32[]{:S(2)}) copy-start(f32[512,96]{0,1:T(8,128)} %param.4) | copy-start | bytes 589828
  88.9 0.9 copy-start.1
  89.8 58.2 %copy-start.3 = (f32[512,96]{0,1:T(8,128)S(1)}, f32[512,96]{0,1:T(8,128)}, u32[]{:S(2)}) copy-start(f32[512,96]{0,1:T(8,128)} %param.5) | copy-start | bytes 589828

commit v5 on v4

--- a/solution.py
+++ b/solution.py
@@ -248,12 +248,13 @@
     return copies
 
 
-def gather_two(basis_ref, fib_ref, s):
+def gather_two(blocks_ref, start_ref, basis_ref, fib_ref, s):
     gx, gy, *_ = place()
     load = pltpu.make_async_copy(fib_ref, s["fib"], s["xc"])
     load.start()
     peers = everyone()
     greet(peers)
+    refine_into(1.0 / (I2 * COLS), blocks_ref, start_ref, basis_ref, s["g"], s["last"], s["inverse"])
     load.wait()
     shrunk = dot(basis_ref[...], s["fib"][...])
     for u in range(GY):
@@ -331,8 +332,8 @@
         copy.wait_send()
 
 
-def second_kernel(basis_ref, fib_ref, f2_ref, g_ref, s):
-    flat, copies = gather_two(basis_ref, fib_ref, s)
+def second_kernel(blocks_ref, start_ref, fib_ref, basis_ref, f2_ref, g_ref, s):
+    flat, copies = gather_two(blocks_ref, start_ref, basis_ref, fib_ref, s)
     f2_ref[...] = flat
     gram_blocks(flat, s["gp"])
     all_reduce(s["gp"], s["total"], s)
@@ -364,8 +365,9 @@
         await_greetings(32)
 
 
-def third_kernel(basis_ref, f2_ref, out_ref, s):
+def third_kernel(blocks_ref, start_ref, f2_ref, basis_ref, out_ref, s):
     greet_senders()
+    refine_into(1.0 / (RANK * COLS), blocks_ref, start_ref, basis_ref, s["g"], s["last"], s["inverse"])
     spread_core(basis_ref[...], f2_ref[...], out_ref, s)
 
 
@@ -375,17 +377,21 @@
     **{"as": DMA((2, 15)), "ar": DMA((2, 15))},
 )
 SECOND = REDUCE | dict(
+    g=pltpu.VMEM((I1, I1), jnp.float32), last=pltpu.VMEM((RANK, I1), jnp.float32),
+    inverse=pltpu.VMEM((RANK, 128), jnp.float32),
     fib=pltpu.VMEM((I1, COLS), jnp.float32), xc=DMA,
     st=pltpu.VMEM((GY, 3, COLS), jnp.float32), f2=pltpu.VMEM((GY, 3, COLS), jnp.float32),
     bs=DMA((31,)), br=DMA((31,)),
 )
 THIRD = dict(
+    g=pltpu.VMEM((I1, I1), jnp.float32), last=pltpu.VMEM((RANK, I1), jnp.float32),
+    inverse=pltpu.VMEM((RANK, 128), jnp.float32),
     cs=pltpu.VMEM((GY, 3, 128), jnp.float32), ro=pltpu.VMEM((GX, 2, 3, 128), jnp.float32),
     ks=DMA((32,)), kr=DMA((GX, 2)),
 )
 
 VMEM = pl.BlockSpec(memory_space=pltpu.VMEM)
-ANY = pl.BlockSpec(memory_space=pl.ANY)
+ANY = pl.BlockSpec(memory_space=pltpu.HBM)
 
 
 def exchange(kernel, name, ident, ins, outs, scratch):
@@ -486,7 +492,7 @@
     return jnp.concatenate(result, axis=0)
 
 
-def refine_kernel(scale, blocks_ref, start_ref, out_ref, g_ref):
+def refine_into(scale, blocks_ref, start_ref, out_ref, g_ref, last_ref, inverse_ref):
     for n, (p, q) in enumerate(BLOCKS):
         block = blocks_ref[128 * n : 128 * (n + 1)] * scale
         g_ref[128 * p : 128 * (p + 1), 128 * q : 128 * (q + 1)] = block
@@ -505,33 +511,23 @@
             return lambda: ahead.append(dot(images, g_ref[:, 256 * n : 256 * (n + 1)]))
 
         inverse = factor(images, [column(n) for n in range(2)])
+        last_ref[...] = images
+        inverse_ref[...] = inverse
         return dot(inverse, jnp.concatenate([jnp.concatenate(ahead, axis=1), pad], axis=0))
 
-    images = dot(start_ref[...], g_ref[...])
-    images = lax.fori_loop(0, ITERS - 1, sweep, images)
-    out_ref[...] = dot(factor(images), jnp.concatenate([images, pad], axis=0))
-
-
-def refine(blocks, start_t, scale, name):
-    vmem = pl.BlockSpec(memory_space=pltpu.VMEM)
-    return pl.pallas_call(
-        functools.partial(refine_kernel, scale),
-        out_shape=jax.ShapeDtypeStruct((RANK, 512), jnp.float32),
-        in_specs=[vmem] * 2,
-        out_specs=vmem,
-        scratch_shapes=[pltpu.VMEM((512, 512), jnp.float32)],
-        compiler_params=pltpu.CompilerParams(vmem_limit_bytes=32 * 1024 * 1024),
-        name=name,
-    )(blocks, start_t)
+    lax.fori_loop(0, ITERS, sweep, dot(start_ref[...], g_ref[...]))
+    out_ref[...] = dot(inverse_ref[...], jnp.concatenate([last_ref[...], pad], axis=0))
 
 
 def body(snapshot, start_one, start_two):
     start_two = start_two.reshape(GY, 16, RANK).transpose(2, 1, 0).reshape(RANK, I2)
     fibers, blocks = exchange(first_kernel, "first", 0, [ANY], [(I1, COLS), (GROWS, 128)], FIRST)(snapshot)
-    basis_one = refine(blocks, start_one.T, 1.0 / (I2 * COLS), "refine_one")
-    fibers_two, blocks = exchange(second_kernel, "second", 1, [VMEM, ANY], [(I2, 128), (GROWS, 128)], SECOND)(basis_one, fibers)
-    basis_two = refine(blocks, start_two, 1.0 / (RANK * COLS), "refine_two")
-    core_tensor = exchange(third_kernel, "third", 2, [VMEM, VMEM], [(6, 3, COLS)], THIRD)(basis_two, fibers_two)
+    basis_one, fibers_two, blocks = exchange(
+        second_kernel, "second", 1, [VMEM, VMEM, ANY], [(RANK, I1), (I2, 128), (GROWS, 128)], SECOND
+    )(blocks, start_one.T, fibers)
+    basis_two, core_tensor = exchange(
+        third_kernel, "third", 2, [VMEM] * 3, [(RANK, I2), (6, 3, COLS)], THIRD
+    )(blocks, start_two, fibers_two)
     basis_two = basis_two.reshape(RANK, 16, GY).transpose(2, 1, 0).reshape(I2, RANK)
     return (basis_one.T, basis_two, core_tensor)
 

time: 187 us -> 175 us (0.936)
  the two profiles are of different devices: /device:TPU:5 before, /device:TPU:21 now
where the time goes in v5:
time: 175 us
  Pallas kernels  171 us (98%)
  local copies, waits for them, and re-layouts  3.84 us (2%)
    pallas_call x3, Pallas kernels, call(): pl.pallas_call(body, out_shape=shapes[0] if single else shapes, in_specs=...  171 us

profile of v5, /device:TPU:21, one launch (start us, length us, event | category | flops | bytes accessed | tf_op | source)
XLA Modules:
  0.0 175.1 jit_solution(4543940948213164052)
XLA Ops:
  0.6 0.0 copy-start
  0.6 1.1 copy-done
  1.8 0.0 copy-start.1
  1.8 65.6 %first.1 = (f32[512,384]{1,0:T(8,128)S(1)}, f32[1280,128]{1,0:T(8,128)S(1)}) custom-call(f32[32,16,384]{2,1,0:T(8,128)S(1)} %copy-done), custom_call_target="tpu_custom_call" | custom-call | tf_op jit(solution)/shard_map/first/pallas_call | solution.py:405
  67.4 0.0 copy-done.1
  67.4 0.0 copy-start.2
  67.4 70.0 %second.1 = (f32[96,512]{1,0:T(8,128)S(1)}, f32[512,128]{1,0:T(8,128)S(1)}, f32[1280,128]{1,0:T(8,128)S(1)}) custom-call(f32[1280,128]{1,0:T(8,128)S(1)} %get-tuple-element.10.refs_0_, f32[96,512]{1,0:T(8,128)S(1)} %bitcast.10, f32[512,384]{1,0:T(8,128)S(1)} %get-tuple-element.11.refs_2_), custom_call_target="tpu_custom_call" | custom-call | tf_op jit(solution)/shard_map/second/pallas_call | solution.py:405
  137.4 0.0 copy-done.2
  137.4 0.1 copy.8
  137.5 0.1 copy.9
  137.6 0.1 copy.10.refs_1_
  137.7 35.0 %third.1 = (f32[96,512]{1,0:T(8,128)S(1)}, f32[6,3,384]{2,1,0:T(4,128)S(1)}) custom-call(f32[1280,128]{1,0:T(8,128)S(1)} %get-tuple-element.13.refs_0_, f32[96,512]{1,0:T(8,128)S(1)} %copy.10.refs_1_, f32[512,128]{1,0:T(8,128)S(1)} %get-tuple-element.14.refs_2_), custom_call_target="tpu_custom_call" | custom-call | tf_op jit(solution)/shard_map/third/pallas_call | solution.py:405
  172.7 0.1 copy.11
  172.9 0.2 copy.12
  173.0 0.8 copy.13
  173.8 0.7 copy.16
  174.5 0.6 copy.17
Async XLA Ops:
  0.6 1.1 copy-start
  1.8 65.6 %copy-start.1 = (f32[512,96]{0,1:T(8,128)S(1)}, f32[512,96]{0,1:T(8,128)}, u32[]{:S(2)}) copy-start(f32[512,96]{0,1:T(8,128)} %param.4) | copy-start | bytes 589828
  67.4 70.0 %copy-start.2 = (f32[512,96]{0,1:T(8,128)S(1)}, f32[512,96]{0,1:T(8,128)}, u32[]{:S(2)}) copy-start(f32[512,96]{0,1:T(8,128)} %param.5) | copy-start | bytes 589828

commit v6 on v5

--- a/solution.py
+++ b/solution.py
@@ -223,6 +223,7 @@
     load.start()
     peers = everyone()
     greet(peers)
+    greet_senders()
     load.wait()
     copies = []
     for half in range(2):
@@ -232,7 +233,7 @@
             for g, tile in enumerate(swap_granules([s["x"][rows, j, lanes] for j in range(16)])):
                 s["xs"][g, rows, lanes] = tile
         if half == 0:
-            await_greetings(len(peers))
+            await_everyone(len(peers))
         rows = pl.ds(16 * half, 16)
         for d in range(1, GX):
             peer = gx_peer(d)
@@ -248,18 +249,11 @@
     return copies
 
 
-def gather_two(blocks_ref, start_ref, basis_ref, fib_ref, s):
+def gather_two(basis_ref, fibers, s):
     gx, gy, *_ = place()
-    load = pltpu.make_async_copy(fib_ref, s["fib"], s["xc"])
-    load.start()
-    peers = everyone()
-    greet(peers)
-    refine_into(1.0 / (I2 * COLS), blocks_ref, start_ref, basis_ref, s["g"], s["last"], s["inverse"])
-    load.wait()
-    shrunk = dot(basis_ref[...], s["fib"][...])
+    shrunk = dot(basis_ref[...], fibers)
     for u in range(GY):
         s["st"][u] = shrunk[3 * u : 3 * (u + 1)]
-    await_greetings(len(peers))
     copies = []
     for d in range(1, GY):
         peer = gy_peer(d)
@@ -280,7 +274,6 @@
     core = dot(basis, columns)
     for u in range(GY):
         s["cs"][u] = core[3 * u : 3 * (u + 1)]
-    await_senders()
 
     def copy(d):
         u = lax.bitwise_xor(gy, d)
@@ -321,27 +314,6 @@
         copy(d).wait_send()
 
 
-def first_kernel(x_ref, fib_ref, g_ref, s):
-    copies = gather_one(x_ref, s)
-    flat = s["fib"][...].reshape(I1, COLS)
-    fib_ref[...] = flat
-    gram_blocks(flat, s["gp"])
-    all_reduce(s["gp"], s["total"], s)
-    g_ref[...] = s["total"][...]
-    for copy in copies:
-        copy.wait_send()
-
-
-def second_kernel(blocks_ref, start_ref, fib_ref, basis_ref, f2_ref, g_ref, s):
-    flat, copies = gather_two(blocks_ref, start_ref, basis_ref, fib_ref, s)
-    f2_ref[...] = flat
-    gram_blocks(flat, s["gp"])
-    all_reduce(s["gp"], s["total"], s)
-    g_ref[...] = s["total"][...]
-    for copy in copies:
-        copy.wait_send()
-
-
 def greet_senders():
     gx, gy, *_ = place()
     barrier = pltpu.get_barrier_semaphore()
@@ -353,41 +325,46 @@
             pl.semaphore_signal(barrier, inc=1, device_id=(lax.rem(gx + k, GX), 2 * gx + h), device_id_type=MESH)
 
 
-def await_senders():
+def await_everyone(count):
     gx, gy, *_ = place()
 
     @pl.when(lax.div(gy, 2) == gx)
     def _():
-        await_greetings(31)
+        await_greetings(count + 31)
 
     @pl.when(lax.div(gy, 2) != gx)
     def _():
-        await_greetings(32)
-
-
-def third_kernel(blocks_ref, start_ref, f2_ref, basis_ref, out_ref, s):
-    greet_senders()
-    refine_into(1.0 / (RANK * COLS), blocks_ref, start_ref, basis_ref, s["g"], s["last"], s["inverse"])
-    spread_core(basis_ref[...], f2_ref[...], out_ref, s)
-
-
-FIRST = REDUCE | dict(
+        await_greetings(count + 32)
+
+
+def whole_kernel(x_ref, start_one_ref, start_two_ref, one_ref, two_ref, core_ref, s):
+    room = (s["g"], s["last"], s["inverse"])
+    copies = gather_one(x_ref, s)
+    flat = s["fib"][...].reshape(I1, COLS)
+    gram_blocks(flat, s["one"]["gp"])
+    all_reduce(s["one"]["gp"], s["one"]["total"], s["one"])
+    refine_into(1.0 / (I2 * COLS), s["one"]["total"], start_one_ref, one_ref, *room)
+    flat, more = gather_two(one_ref, flat, s)
+    s["columns"][...] = flat
+    gram_blocks(flat, s["two"]["gp"])
+    all_reduce(s["two"]["gp"], s["two"]["total"], s["two"])
+    refine_into(1.0 / (RANK * COLS), s["two"]["total"], start_two_ref, two_ref, *room)
+    spread_core(two_ref[...], s["columns"][...], core_ref, s)
+    for copy in copies + more:
+        copy.wait_send()
+
+
+WHOLE = dict(
+    one=REDUCE, two=REDUCE,
     x=pltpu.VMEM((32, 16, COLS), jnp.float32), xc=DMA,
     xs=pltpu.VMEM((GX, 32, COLS), jnp.float32), fib=pltpu.VMEM((GX, 32, COLS), jnp.float32),
-    **{"as": DMA((2, 15)), "ar": DMA((2, 15))},
-)
-SECOND = REDUCE | dict(
+    st=pltpu.VMEM((GY, 3, COLS), jnp.float32), f2=pltpu.VMEM((GY, 3, COLS), jnp.float32),
+    columns=pltpu.VMEM((I2, 128), jnp.float32),
+    cs=pltpu.VMEM((GY, 3, 128), jnp.float32), ro=pltpu.VMEM((GX, 2, 3, 128), jnp.float32),
     g=pltpu.VMEM((I1, I1), jnp.float32), last=pltpu.VMEM((RANK, I1), jnp.float32),
     inverse=pltpu.VMEM((RANK, 128), jnp.float32),
-    fib=pltpu.VMEM((I1, COLS), jnp.float32), xc=DMA,
-    st=pltpu.VMEM((GY, 3, COLS), jnp.float32), f2=pltpu.VMEM((GY, 3, COLS), jnp.float32),
-    bs=DMA((31,)), br=DMA((31,)),
-)
-THIRD = dict(
-    g=pltpu.VMEM((I1, I1), jnp.float32), last=pltpu.VMEM((RANK, I1), jnp.float32),
-    inverse=pltpu.VMEM((RANK, 128), jnp.float32),
-    cs=pltpu.VMEM((GY, 3, 128), jnp.float32), ro=pltpu.VMEM((GX, 2, 3, 128), jnp.float32),
     ks=DMA((32,)), kr=DMA((GX, 2)),
+    bs=DMA((31,)), br=DMA((31,)), **{"as": DMA((2, 15)), "ar": DMA((2, 15))},
 )
 
 VMEM = pl.BlockSpec(memory_space=pltpu.VMEM)
@@ -521,13 +498,10 @@
 
 def body(snapshot, start_one, start_two):
     start_two = start_two.reshape(GY, 16, RANK).transpose(2, 1, 0).reshape(RANK, I2)
-    fibers, blocks = exchange(first_kernel, "first", 0, [ANY], [(I1, COLS), (GROWS, 128)], FIRST)(snapshot)
-    basis_one, fibers_two, blocks = exchange(
-        second_kernel, "second", 1, [VMEM, VMEM, ANY], [(RANK, I1), (I2, 128), (GROWS, 128)], SECOND
-    )(blocks, start_one.T, fibers)
-    basis_two, core_tensor = exchange(
-        third_kernel, "third", 2, [VMEM] * 3, [(RANK, I2), (6, 3, COLS)], THIRD
-    )(blocks, start_two, fibers_two)
+    shapes = [(RANK, I1), (RANK, I2), (6, 3, COLS)]
+    basis_one, basis_two, core_tensor = exchange(whole_kernel, "whole", 0, [ANY, VMEM, VMEM], shapes, WHOLE)(
+        snapshot, start_one.T, start_two
+    )
     basis_two = basis_two.reshape(RANK, 16, GY).transpose(2, 1, 0).reshape(I2, RANK)
     return (basis_one.T, basis_two, core_tensor)
 

time: 175 us -> 173 us (0.989)
  the two profiles are of different devices: /device:TPU:21 before, /device:TPU:1 now
where the time goes in v6:
time: 173 us; the launch traced here: 171 us
  Pallas kernels  165 us (95%)
  local copies, waits for them, and re-layouts  4.49 us (3%)
    pallas_call x1, Pallas kernels, call(): pl.pallas_call(body, out_shape=shapes[0] if single else shapes, in_specs=...  165 us
    unnamed x8, local copies, waits for them, and re-layouts  4 us

profile of v6, /device:TPU:1, one launch (start us, length us, event | category | flops | bytes accessed | tf_op | source)
XLA Modules:
  0.0 170.6 jit_solution(16358914981517932764)
XLA Ops:
  0.6 0.0 copy-start
  0.6 1.1 copy.8
  1.8 0.1 copy.9
  1.9 0.0 copy-start.1
  1.9 0.1 copy.10.refs_2_
  2.0 0.0 copy-done
  2.0 0.8 copy-done.1
  2.8 165.4 %whole.1 = (f32[96,512]{1,0:T(8,128)S(1)}, f32[96,512]{1,0:T(8,128)S(1)}, f32[6,3,384]{2,1,0:T(4,128)S(1)}) custom-call(f32[32,16,384]{2,1,0:T(8,128)S(1)} %copy-done, f32[96,512]{1,0:T(8,128)S(1)} %bitcast.10, f32[96,512]{1,0:T(8,128)S(1)} %copy.10.refs_2_), custom_call_target="tpu_custom_call" | custom-call | tf_op jit(solution)/shard_map/whole/pallas_call | solution.py:382
  168.2 0.1 copy.11
  168.3 0.2 copy.12
  168.5 0.8 copy.13
  169.3 0.7 copy.16
  170.0 0.6 copy.17
Async XLA Ops:
  0.6 1.4 copy-start
  1.9 0.9 copy-start.1
